TPU v7x, 512 devices: a whole 4x8x8 slice. The times are simulated.
512 devices in a mesh: pts: 512 (over x, y, z, core).
Axes of the slice: x: 4, y: 8, z: 8, core: 2. Of those that a mesh axis runs over, the one named last changes fastest.
Arguments:
- coords: int32 [2, 262144], P(None, 'pts'), may hold values from 0 to 262143, as said below
- probes: int32 [16, 262144], P(None, 'pts'), may hold values from 0 to 1
- u_bases: bfloat16 [1600, 262144], P(None, 'pts')
- v_bases: bfloat16 [1600, 262144], P(None, 'pts')
Outputs:
- forward: float32 [16, 262144], P(None, 'pts')
- transposed: float32 [16, 262144], P(None, 'pts')
Inputs may be any that keep to these rules, and one draw needn't show every extreme that they name: `coords`: points are laid leaf by leaf; leaf k's point i sits in grid cell (k * 16 + i % 16, i // 16); each component is 16 times its cell index plus a jitter of 0 to 15; the first point's jitter is 0 and the last point's is 15.
All inputs are finite; a program needn't handle non-finite values.
Results may differ from a plain program's by a relative error of at most 0.0028.
Values may be sent and summed in bfloat16 or wider, within the bound.
A program may use at most 64 MiB of HBM per device.

v0:
```python
import jax
import jax.numpy as jnp
from jax import lax
from jax.sharding import PartitionSpec as P

LEAF = 256
RANK_UNIT = 64


factor_list = (1, 1, 1, 1, 2, 2, 4, 4, 8, 8)
cell_units = 16.0
length_scale = 4.0
root_three = 1.7320508075688772
nugget = 0.1


def partner(x, axis, apart):
    return lax.ppermute(x, axis, [(i, i ^ 1 << apart) for i in range(lax.axis_size(axis))])


def matern_leaf(points):
    spots = points.astype(jnp.float32) / cell_units
    delta_x = spots[0][:, None] - spots[0][None, :]
    delta_y = spots[1][:, None] - spots[1][None, :]
    scaled = root_three * jnp.sqrt(delta_x * delta_x + delta_y * delta_y) / length_scale
    kernel = (1.0 + scaled) * jnp.exp(-scaled) + nugget * jnp.eye(
        points.shape[1], dtype=jnp.float32
    )
    return kernel.astype(jnp.bfloat16)


def sibling_sums(coef_list, level_bits):
    result = []
    for level in range(level_bits):
        partial_value = coef_list[level]
        for lower in range(level):
            partial_value = partial_value + partner(partial_value, "pts", lower)
        result.append(partner(partial_value.astype(jnp.bfloat16), "pts", level))
    return result


def shards(coords, probes, u_bases, v_bases):
    level_bits = lax.axis_size("pts").bit_length() - 1
    widths = [RANK_UNIT * factor_list[level] for level in range(level_bits)]
    points_here = coords.shape[1]
    probe_count = probes.shape[0]
    leaf_count = points_here // LEAF
    sign_rows = (2 * probes - 1).astype(jnp.bfloat16)
    leaf_points = coords.reshape(2, leaf_count, LEAF).transpose(1, 0, 2)
    blocks = jax.vmap(matern_leaf)(leaf_points)
    leaf_signs = sign_rows.reshape(probe_count, leaf_count, LEAF)
    near = jnp.einsum("pnl,nlm->pnm", leaf_signs, blocks, preferred_element_type=jnp.float32)
    near = near.reshape(probe_count, points_here)
    local_u = u_bases[:RANK_UNIT].reshape(RANK_UNIT, leaf_count, LEAF)
    local_v = v_bases[:RANK_UNIT].reshape(RANK_UNIT, leaf_count, LEAF)

    def local_term(contract_rows, apply_rows):
        coef = jnp.einsum(
            "pnl,rnl->pnr", leaf_signs, contract_rows, preferred_element_type=jnp.float32
        )
        paired = coef.reshape(probe_count, leaf_count // 2, 2, RANK_UNIT)
        sibling = (
            jnp.flip(paired, axis=2)
            .reshape(probe_count, leaf_count, RANK_UNIT)
            .astype(jnp.bfloat16)
        )
        applied = jnp.einsum(
            "pnr,rnl->pnl", sibling, apply_rows, preferred_element_type=jnp.float32
        )
        return applied.reshape(probe_count, points_here)

    cross_u = u_bases[RANK_UNIT:]
    cross_v = v_bases[RANK_UNIT:]
    contract_dims = (((1,), (1,)), ((), ()))
    forward_coef = lax.dot_general(
        sign_rows, cross_v, contract_dims, preferred_element_type=jnp.float32
    )
    transpose_coef = lax.dot_general(
        sign_rows, cross_u, contract_dims, preferred_element_type=jnp.float32
    )

    def split_levels(joined):
        pieces = []
        start = 0
        for width in widths:
            pieces.append(joined[:, start : start + width])
            start = start + width
        return pieces

    forward_sib = jnp.concatenate(sibling_sums(split_levels(forward_coef), level_bits), axis=1)
    transpose_sib = jnp.concatenate(sibling_sums(split_levels(transpose_coef), level_bits), axis=1)
    far_forward = jnp.dot(forward_sib, cross_u, preferred_element_type=jnp.float32)
    far_transpose = jnp.dot(transpose_sib, cross_v, preferred_element_type=jnp.float32)
    forward = near + local_term(local_v, local_u) + far_forward
    transposed = near + local_term(local_u, local_v) + far_transpose
    return (forward, transposed)


def solution(mesh):
    return jax.shard_map(
        shards,
        mesh=mesh,
        in_specs=(P(None, "pts"), P(None, "pts"), P(None, "pts"), P(None, "pts")),
        out_specs=(P(None, "pts"), P(None, "pts")),
        check_vma=False,
    )
```

profile of v0, /device:TPU:1, one launch (start us, length us, event | category | flops | bytes accessed | tf_op | source)
XLA Modules:
  0.0 322.5 jit_solution(17457941004248472606)
XLA Ops:
  3.5 8.9 %collective-permute-start.66 = (f32[16,256]{1,0:T(8,128)S(1)}, f32[16,256]{1,0:T(8,128)S(1)}, u32[]{:S(2)}, u32[]{:S(2)}) collective-permute-start(f32[16,256]{1,0:T(8,128)S(1)} %get-tuple-element.5), channel_id=1, source_target_pairs={{0,1},{1,0},{2,3},{3,2},{4,5},{5,4},{6,7},{7,6},{8,9},{9,8},{10,11... | collective-permute-start | bytes 49160 | tf_op jit(solution)/shard_map/ppermute | solution.py:18
  43.3 3.4 %collective-permute-start.49 = (f32[16,64]{1,0:T(8,128)S(1)}, f32[16,64]{1,0:T(8,128)S(1)}, u32[]{:S(2)}, u32[]{:S(2)}) collective-permute-start(f32[16,64]{1,0:T(8,128)S(1)} %get-tuple-element.12), channel_id=1, source_target_pairs={{0,2},{1,3},{2,0},{3,1},{4,6},{5,7},{6,4},{7,5},{8,10},{9,11},{10,... | collective-permute-start | bytes 12296 | tf_op jit(solution)/shard_map/ppermute | solution.py:18
  47.7 3.4 %collective-permute-start.4 = (f32[16,64]{1,0:T(8,128)S(1)}, f32[16,64]{1,0:T(8,128)S(1)}, u32[]{:S(2)}, u32[]{:S(2)}) collective-permute-start(f32[16,64]{1,0:T(8,128)S(1)} %get-tuple-element.26), channel_id=1, source_target_pairs={{0,2},{1,3},{2,0},{3,1},{4,6},{5,7},{6,4},{7,5},{8,10},{9,11},{10,... | collective-permute-start | bytes 12296 | tf_op jit(solution)/shard_map/ppermute | solution.py:18
  55.6 4.7 %collective-permute-start.28 = (f32[16,256]{1,0:T(8,128)S(1)}, f32[16,256]{1,0:T(8,128)S(1)}, u32[]{:S(2)}, u32[]{:S(2)}) collective-permute-start(f32[16,256]{1,0:T(8,128)S(1)} %get-tuple-element.18), channel_id=1, source_target_pairs={{0,1},{1,0},{2,3},{3,2},{4,5},{5,4},{6,7},{7,6},{8,9},{9,8},{10,11... | collective-permute-start | bytes 49160 | tf_op jit(solution)/shard_map/ppermute | solution.py:18
  67.9 3.0 collective-permute-start.56
  73.2 3.0 collective-permute-start.11
  76.3 5.1 %collective-permute-start.81 = (f32[16,512]{1,0:T(8,128)S(1)}, f32[16,512]{1,0:T(8,128)S(1)}, u32[]{:S(2)}, u32[]{:S(2)}) collective-permute-start(f32[16,512]{1,0:T(8,128)S(1)} %slice.119), channel_id=1, source_target_pairs={{0,1},{1,0},{2,3},{3,2},{4,5},{5,4},{6,7},{7,6},{8,9},{9,8},{10,11... | collective-permute-start | bytes 98312 | tf_op jit(solution)/shard_map/ppermute | solution.py:18
  84.2 3.4 %collective-permute-start.57 = (f32[16,128]{1,0:T(8,128)S(1)}, f32[16,128]{1,0:T(8,128)S(1)}, u32[]{:S(2)}, u32[]{:S(2)}) collective-permute-start(f32[16,128]{1,0:T(8,128)S(1)} %add.305), channel_id=1, source_target_pairs={{0,4},{1,5},{2,6},{3,7},{4,0},{5,1},{6,2},{7,3},{8,12},{9,13},{10,... | collective-permute-start | bytes 24584 | tf_op jit(solution)/shard_map/ppermute | solution.py:18
  90.4 3.4 %collective-permute-start.12 = (f32[16,128]{1,0:T(8,128)S(1)}, f32[16,128]{1,0:T(8,128)S(1)}, u32[]{:S(2)}, u32[]{:S(2)}) collective-permute-start(f32[16,128]{1,0:T(8,128)S(1)} %add.266), channel_id=1, source_target_pairs={{0,4},{1,5},{2,6},{3,7},{4,0},{5,1},{6,2},{7,3},{8,12},{9,13},{10,... | collective-permute-start | bytes 24584 | tf_op jit(solution)/shard_map/ppermute | solution.py:18
  93.9 3.0 collective-permute-start.36
  96.9 3.6 %collective-permute-start.74 = (f32[16,256]{1,0:T(8,128)S(1)}, f32[16,256]{1,0:T(8,128)S(1)}, u32[]{:S(2)}, u32[]{:S(2)}) collective-permute-start(f32[16,256]{1,0:T(8,128)S(1)} %get-tuple-element.2), channel_id=1, source_target_pairs={{0,2},{1,3},{2,0},{3,1},{4,6},{5,7},{6,4},{7,5},{8,10},{9,11},{10,... | collective-permute-start | bytes 49160 | tf_op jit(solution)/shard_map/ppermute | solution.py:18
  102.6 3.4 %collective-permute-start.29 = (f32[16,256]{1,0:T(8,128)S(1)}, f32[16,256]{1,0:T(8,128)S(1)}, u32[]{:S(2)}, u32[]{:S(2)}) collective-permute-start(f32[16,256]{1,0:T(8,128)S(1)} %get-tuple-element.16), channel_id=1, source_target_pairs={{0,2},{1,3},{2,0},{3,1},{4,6},{5,7},{6,4},{7,5},{8,10},{9,11},{10,... | collective-permute-start | bytes 49160 | tf_op jit(solution)/shard_map/ppermute | solution.py:18
  107.9 6.5 %collective-permute-start.63 = (f32[16,128]{1,0:T(8,128)S(1)}, f32[16,128]{1,0:T(8,128)S(1)}, u32[]{:S(2)}, u32[]{:S(2)}) collective-permute-start(f32[16,128]{1,0:T(8,128)S(1)} %add.310), channel_id=1, source_target_pairs={{0,8},{1,9},{2,10},{3,11},{4,12},{5,13},{6,14},{7,15},{8,0},{9,1},... | collective-permute-start | bytes 24584 | tf_op jit(solution)/shard_map/ppermute | solution.py:18
  117.2 3.2 collective-permute-start.75
  120.4 3.0 collective-permute-start.68
  123.4 3.2 collective-permute-start.30
  126.6 7.3 %collective-permute-start.18 = (f32[16,128]{1,0:T(8,128)S(1)}, f32[16,128]{1,0:T(8,128)S(1)}, u32[]{:S(2)}, u32[]{:S(2)}) collective-permute-start(f32[16,128]{1,0:T(8,128)S(1)} %add.271), channel_id=1, source_target_pairs={{0,8},{1,9},{2,10},{3,11},{4,12},{5,13},{6,14},{7,15},{8,0},{9,1},... | collective-permute-start | bytes 24584 | tf_op jit(solution)/shard_map/ppermute | solution.py:18
  138.1 4.2 %collective-permute-start.23 = (f32[16,256]{1,0:T(8,128)S(1)}, f32[16,256]{1,0:T(8,128)S(1)}, u32[]{:S(2)}, u32[]{:S(2)}) collective-permute-start(f32[16,256]{1,0:T(8,128)S(1)} %add.275), channel_id=1, source_target_pairs={{0,4},{1,5},{2,6},{3,7},{4,0},{5,1},{6,2},{7,3},{8,12},{9,13},{10,... | collective-permute-start | bytes 49160 | tf_op jit(solution)/shard_map/ppermute | solution.py:18
  142.3 5.3 %collective-permute-start.76 = (f32[16,256]{1,0:T(8,128)S(1)}, f32[16,256]{1,0:T(8,128)S(1)}, u32[]{:S(2)}, u32[]{:S(2)}) collective-permute-start(f32[16,256]{1,0:T(8,128)S(1)} %add.321), channel_id=1, source_target_pairs={{0,8},{1,9},{2,10},{3,11},{4,12},{5,13},{6,14},{7,15},{8,0},{9,1},... | collective-permute-start | bytes 49160 | tf_op jit(solution)/shard_map/ppermute | solution.py:18
  147.6 3.2 collective-permute-start.64
  150.8 3.2 collective-permute-start.37
  154.0 3.0 collective-permute-start.69
  157.1 6.2 %collective-permute-start.31 = (f32[16,256]{1,0:T(8,128)S(1)}, f32[16,256]{1,0:T(8,128)S(1)}, u32[]{:S(2)}, u32[]{:S(2)}) collective-permute-start(f32[16,256]{1,0:T(8,128)S(1)} %add.282), channel_id=1, source_target_pairs={{0,8},{1,9},{2,10},{3,11},{4,12},{5,13},{6,14},{7,15},{8,0},{9,1},... | collective-permute-start | bytes 49160 | tf_op jit(solution)/shard_map/ppermute | solution.py:18
  163.3 3.0 collective-permute-start.24
  171.3 3.2 collective-permute-start.77
  176.6 3.4 %collective-permute-start.38 = (f32[16,512]{1,0:T(8,128)S(1)}, f32[16,512]{1,0:T(8,128)S(1)}, u32[]{:S(2)}, u32[]{:S(2)}) collective-permute-start(f32[16,512]{1,0:T(8,128)S(1)} %add.288), channel_id=1, source_target_pairs={{0,4},{1,5},{2,6},{3,7},{4,0},{5,1},{6,2},{7,3},{8,12},{9,13},{10,... | collective-permute-start | bytes 98312 | tf_op jit(solution)/shard_map/ppermute | solution.py:18
  180.1 3.2 collective-permute-start.32
  185.4 4.2 %collective-permute-start.71 = (f32[16,256]{1,0:T(8,128)S(1)}, f32[16,256]{1,0:T(8,128)S(1)}, u32[]{:S(2)}, u32[]{:S(2)}) collective-permute-start(f32[16,256]{1,0:T(8,128)S(1)} %add.317), channel_id=1, source_target_pairs={{0,32},{1,33},{2,34},{3,35},{4,36},{5,37},{6,38},{7,39},{8,40},{9,... | collective-permute-start | bytes 49160 | tf_op jit(solution)/shard_map/ppermute | solution.py:18
  189.7 6.5 %collective-permute-start.84 = (f32[16,512]{1,0:T(8,128)S(1)}, f32[16,512]{1,0:T(8,128)S(1)}, u32[]{:S(2)}, u32[]{:S(2)}) collective-permute-start(f32[16,512]{1,0:T(8,128)S(1)} %add.328), channel_id=1, source_target_pairs={{0,8},{1,9},{2,10},{3,11},{4,12},{5,13},{6,14},{7,15},{8,0},{9,1},... | collective-permute-start | bytes 98312 | tf_op jit(solution)/shard_map/ppermute | solution.py:18
  198.9 10.8 %collective-permute-start.45 = (bf16[16,64]{1,0:T(8,128)(2,1)S(1)}, bf16[16,64]{1,0:T(8,128)(2,1)S(1)}, u32[]{:S(2)}, u32[]{:S(2)}) collective-permute-start(bf16[16,64]{1,0:T(8,128)(2,1)S(1)} %slice.152), channel_id=1, source_target_pairs={{0,1},{1,0},{2,3},{3,2},{4,5},{5,4},{6,7},{7,6},{8,9},{9,8},{10,11... | collective-permute-start | bytes 6152 | tf_op jit(solution)/shard_map/ppermute | solution.py:18
  211.7 4.2 %collective-permute-start.26 = (f32[16,256]{1,0:T(8,128)S(1)}, f32[16,256]{1,0:T(8,128)S(1)}, u32[]{:S(2)}, u32[]{:S(2)}) collective-permute-start(f32[16,256]{1,0:T(8,128)S(1)} %add.278), channel_id=1, source_target_pairs={{0,32},{1,33},{2,34},{3,35},{4,36},{5,37},{6,38},{7,39},{8,40},{9,... | collective-permute-start | bytes 49160 | tf_op jit(solution)/shard_map/ppermute | solution.py:18
  216.0 3.2 collective-permute-start.85
  223.3 7.5 %collective-permute-start.79 = (f32[16,256]{1,0:T(8,128)S(1)}, f32[16,256]{1,0:T(8,128)S(1)}, u32[]{:S(2)}, u32[]{:S(2)}) collective-permute-start(f32[16,256]{1,0:T(8,128)S(1)} %add.324), channel_id=1, source_target_pairs={{0,64},{1,65},{2,66},{3,67},{4,68},{5,69},{6,70},{7,71},{8,72},{9,... | collective-permute-start | bytes 49160 | tf_op jit(solution)/shard_map/ppermute | solution.py:18
  233.2 3.8 %collective-permute-start.41 = (f32[16,512]{1,0:T(8,128)S(1)}, f32[16,512]{1,0:T(8,128)S(1)}, u32[]{:S(2)}, u32[]{:S(2)}) collective-permute-start(f32[16,512]{1,0:T(8,128)S(1)} %add.291), channel_id=1, source_target_pairs={{0,32},{1,33},{2,34},{3,35},{4,36},{5,37},{6,38},{7,39},{8,40},{9,... | collective-permute-start | bytes 98312 | tf_op jit(solution)/shard_map/ppermute | solution.py:18
  241.3 7.2 %collective-permute-start.87 = (f32[16,512]{1,0:T(8,128)S(1)}, f32[16,512]{1,0:T(8,128)S(1)}, u32[]{:S(2)}, u32[]{:S(2)}) collective-permute-start(f32[16,512]{1,0:T(8,128)S(1)} %add.331), channel_id=1, source_target_pairs={{0,64},{1,65},{2,66},{3,67},{4,68},{5,69},{6,70},{7,71},{8,72},{9,... | collective-permute-start | bytes 98312 | tf_op jit(solution)/shard_map/ppermute | solution.py:18
  253.2 6.8 %collective-permute-start.54 = (bf16[16,64]{1,0:T(8,128)(2,1)S(1)}, bf16[16,64]{1,0:T(8,128)(2,1)S(1)}, u32[]{:S(2)}, u32[]{:S(2)}) collective-permute-start(bf16[16,64]{1,0:T(8,128)(2,1)S(1)} %add_convert_fusion.11), channel_id=1, source_target_pairs={{0,8},{1,9},{2,10},{3,11},{4,12},{5,13},{6,14},{7,15},{8,0},{9,1},... | collective-permute-start | bytes 6152 | tf_op jit(solution)/shard_map/ppermute | solution.py:18
  260.0 3.1 collective-permute-start.88
  263.2 3.0 collective-permute-start.59
  266.2 4.2 %collective-permute-start.65 = (bf16[16,128]{1,0:T(8,128)(2,1)S(1)}, bf16[16,128]{1,0:T(8,128)(2,1)S(1)}, u32[]{:S(2)}, u32[]{:S(2)}) collective-permute-start(bf16[16,128]{1,0:T(8,128)(2,1)S(1)} %add_convert_fusion.9), channel_id=1, source_target_pairs={{0,32},{1,33},{2,34},{3,35},{4,36},{5,37},{6,38},{7,39},{8,40},{9,... | collective-permute-start | bytes 12296 | tf_op jit(solution)/shard_map/ppermute | solution.py:18
  270.5 4.8 %collective-permute-start.72 = (bf16[16,256]{1,0:T(8,128)(2,1)S(1)}, bf16[16,256]{1,0:T(8,128)(2,1)S(1)}, u32[]{:S(2)}, u32[]{:S(2)}) collective-permute-start(bf16[16,256]{1,0:T(8,128)(2,1)S(1)} %add_convert_fusion.6), channel_id=1, source_target_pairs={{0,64},{1,65},{2,66},{3,67},{4,68},{5,69},{6,70},{7,71},{8,72},{9,... | collective-permute-start | bytes 24584 | tf_op jit(solution)/shard_map/ppermute | solution.py:18
  277.4 3.1 collective-permute-start.43
  280.6 7.8 %collective-permute-start = (bf16[16,64]{1,0:T(8,128)(2,1)S(1)}, bf16[16,64]{1,0:T(8,128)(2,1)S(1)}, u32[]{:S(2)}, u32[]{:S(2)}) collective-permute-start(bf16[16,64]{1,0:T(8,128)(2,1)S(1)} %slice.153), channel_id=1, source_target_pairs={{0,1},{1,0},{2,3},{3,2},{4,5},{5,4},{6,7},{7,6},{8,9},{9,8},{10,11... | collective-permute-start | bytes 6152 | tf_op jit(solution)/shard_map/ppermute | solution.py:18
  288.3 3.1 collective-permute-start.2
  294.0 3.4 %collective-permute-start.9 = (bf16[16,64]{1,0:T(8,128)(2,1)S(1)}, bf16[16,64]{1,0:T(8,128)(2,1)S(1)}, u32[]{:S(2)}, u32[]{:S(2)}) collective-permute-start(bf16[16,64]{1,0:T(8,128)(2,1)S(1)} %add_convert_fusion.16), channel_id=1, source_target_pairs={{0,8},{1,9},{2,10},{3,11},{4,12},{5,13},{6,14},{7,15},{8,0},{9,1},... | collective-permute-start | bytes 6152 | tf_op jit(solution)/shard_map/ppermute | solution.py:18
  297.4 4.4 %collective-permute-start.89 = (bf16[16,512]{1,0:T(8,128)(2,1)S(1)}, bf16[16,512]{1,0:T(8,128)(2,1)S(1)}, u32[]{:S(2)}, u32[]{:S(2)}) collective-permute-start(bf16[16,512]{1,0:T(8,128)(2,1)S(1)} %add_convert_fusion.2), channel_id=1, source_target_pairs={{0,256},{1,257},{2,258},{3,259},{4,260},{5,261},{6,262},{7,263},{8... | collective-permute-start | bytes 49160 | tf_op jit(solution)/shard_map/ppermute | solution.py:18
  303.5 2.9 collective-permute-start.14
  306.6 3.5 %collective-permute-start.20 = (bf16[16,128]{1,0:T(8,128)(2,1)S(1)}, bf16[16,128]{1,0:T(8,128)(2,1)S(1)}, u32[]{:S(2)}, u32[]{:S(2)}) collective-permute-start(bf16[16,128]{1,0:T(8,128)(2,1)S(1)} %add_convert_fusion.14), channel_id=1, source_target_pairs={{0,32},{1,33},{2,34},{3,35},{4,36},{5,37},{6,38},{7,39},{8,40},{9,... | collective-permute-start | bytes 12296 | tf_op jit(solution)/shard_map/ppermute | solution.py:18
  315.2 4.7 %collective-permute-start.44 = (bf16[16,512]{1,0:T(8,128)(2,1)S(1)}, bf16[16,512]{1,0:T(8,128)(2,1)S(1)}, u32[]{:S(2)}, u32[]{:S(2)}) collective-permute-start(bf16[16,512]{1,0:T(8,128)(2,1)S(1)} %add_convert_fusion.3), channel_id=1, source_target_pairs={{0,256},{1,257},{2,258},{3,259},{4,260},{5,261},{6,262},{7,263},{8... | collective-permute-start | bytes 49160 | tf_op jit(solution)/shard_map/ppermute | solution.py:18
  (234 shorter events, 108.7 us)
Async XLA Ops:
  3.5 64.4 %collective-permute-start.66 = (f32[16,256]{1,0:T(8,128)S(1)}, f32[16,256]{1,0:T(8,128)S(1)}, u32[]{:S(2)}, u32[]{:S(2)}) collective-permute-start(f32[16,256]{1,0:T(8,128)S(1)} %get-tuple-element.5), channel_id=1, source_target_pairs={{0,1},{1,0},{2,3},{3,2},{4,5},{5,4},{6,7},{7,6},{8,9},{9,8},{10,11... | collective-permute-start | bytes 49160 | tf_op jit(solution)/shard_map/ppermute | solution.py:18
  12.4 58.5 %collective-permute-start.73 = (f32[16,256]{1,0:T(8,128)S(1)}, f32[16,256]{1,0:T(8,128)S(1)}, u32[]{:S(2)}, u32[]{:S(2)}) collective-permute-start(f32[16,256]{1,0:T(8,128)S(1)} %get-tuple-element.4), channel_id=1, source_target_pairs={{0,1},{1,0},{2,3},{3,2},{4,5},{5,4},{6,7},{7,6},{8,9},{9,8},{10,11... | collective-permute-start | bytes 49160 | tf_op jit(solution)/shard_map/ppermute | solution.py:18
  34.5 53.1 %collective-permute-start.21 = (f32[16,256]{1,0:T(8,128)S(1)}, f32[16,256]{1,0:T(8,128)S(1)}, u32[]{:S(2)}, u32[]{:S(2)}) collective-permute-start(f32[16,256]{1,0:T(8,128)S(1)} %get-tuple-element.19), channel_id=1, source_target_pairs={{0,1},{1,0},{2,3},{3,2},{4,5},{5,4},{6,7},{7,6},{8,9},{9,8},{10,11... | collective-permute-start | bytes 49160 | tf_op jit(solution)/shard_map/ppermute | solution.py:18
  55.6 34.8 %collective-permute-start.28 = (f32[16,256]{1,0:T(8,128)S(1)}, f32[16,256]{1,0:T(8,128)S(1)}, u32[]{:S(2)}, u32[]{:S(2)}) collective-permute-start(f32[16,256]{1,0:T(8,128)S(1)} %get-tuple-element.18), channel_id=1, source_target_pairs={{0,1},{1,0},{2,3},{3,2},{4,5},{5,4},{6,7},{7,6},{8,9},{9,8},{10,11... | collective-permute-start | bytes 49160 | tf_op jit(solution)/shard_map/ppermute | solution.py:18
  76.3 29.7 %collective-permute-start.81 = (f32[16,512]{1,0:T(8,128)S(1)}, f32[16,512]{1,0:T(8,128)S(1)}, u32[]{:S(2)}, u32[]{:S(2)}) collective-permute-start(f32[16,512]{1,0:T(8,128)S(1)} %slice.119), channel_id=1, source_target_pairs={{0,1},{1,0},{2,3},{3,2},{4,5},{5,4},{6,7},{7,6},{8,9},{9,8},{10,11... | collective-permute-start | bytes 98312 | tf_op jit(solution)/shard_map/ppermute | solution.py:18
  93.9 26.5 %collective-permute-start.36 = (f32[16,512]{1,0:T(8,128)S(1)}, f32[16,512]{1,0:T(8,128)S(1)}, u32[]{:S(2)}, u32[]{:S(2)}) collective-permute-start(f32[16,512]{1,0:T(8,128)S(1)} %slice.110), channel_id=1, source_target_pairs={{0,1},{1,0},{2,3},{3,2},{4,5},{5,4},{6,7},{7,6},{8,9},{9,8},{10,11... | collective-permute-start | bytes 98312 | tf_op jit(solution)/shard_map/ppermute | solution.py:18
  100.6 13.8 %collective-permute-start.67 = (f32[16,256]{1,0:T(8,128)S(1)}, f32[16,256]{1,0:T(8,128)S(1)}, u32[]{:S(2)}, u32[]{:S(2)}) collective-permute-start(f32[16,256]{1,0:T(8,128)S(1)} %get-tuple-element.3), channel_id=1, source_target_pairs={{0,2},{1,3},{2,0},{3,1},{4,6},{5,7},{6,4},{7,5},{8,10},{9,11},{10,... | collective-permute-start | bytes 49160 | tf_op jit(solution)/shard_map/ppermute | solution.py:18
  102.6 14.6 %collective-permute-start.29 = (f32[16,256]{1,0:T(8,128)S(1)}, f32[16,256]{1,0:T(8,128)S(1)}, u32[]{:S(2)}, u32[]{:S(2)}) collective-permute-start(f32[16,256]{1,0:T(8,128)S(1)} %get-tuple-element.16), channel_id=1, source_target_pairs={{0,2},{1,3},{2,0},{3,1},{4,6},{5,7},{6,4},{7,5},{8,10},{9,11},{10,... | collective-permute-start | bytes 49160 | tf_op jit(solution)/shard_map/ppermute | solution.py:18
  105.9 17.4 %collective-permute-start.22 = (f32[16,256]{1,0:T(8,128)S(1)}, f32[16,256]{1,0:T(8,128)S(1)}, u32[]{:S(2)}, u32[]{:S(2)}) collective-permute-start(f32[16,256]{1,0:T(8,128)S(1)} %get-tuple-element.17), channel_id=1, source_target_pairs={{0,2},{1,3},{2,0},{3,1},{4,6},{5,7},{6,4},{7,5},{8,10},{9,11},{10,... | collective-permute-start | bytes 49160 | tf_op jit(solution)/shard_map/ppermute | solution.py:18
  107.9 26.0 %collective-permute-start.63 = (f32[16,128]{1,0:T(8,128)S(1)}, f32[16,128]{1,0:T(8,128)S(1)}, u32[]{:S(2)}, u32[]{:S(2)}) collective-permute-start(f32[16,128]{1,0:T(8,128)S(1)} %add.310), channel_id=1, source_target_pairs={{0,8},{1,9},{2,10},{3,11},{4,12},{5,13},{6,14},{7,15},{8,0},{9,1},... | collective-permute-start | bytes 24584 | tf_op jit(solution)/shard_map/ppermute | solution.py:18
  114.5 21.4 %collective-permute-start.58 = (f32[16,128]{1,0:T(8,128)S(1)}, f32[16,128]{1,0:T(8,128)S(1)}, u32[]{:S(2)}, u32[]{:S(2)}) collective-permute-start(f32[16,128]{1,0:T(8,128)S(1)} %add.306), channel_id=1, source_target_pairs={{0,8},{1,9},{2,10},{3,11},{4,12},{5,13},{6,14},{7,15},{8,0},{9,1},... | collective-permute-start | bytes 24584 | tf_op jit(solution)/shard_map/ppermute | solution.py:18
  120.4 17.7 %collective-permute-start.68 = (f32[16,256]{1,0:T(8,128)S(1)}, f32[16,256]{1,0:T(8,128)S(1)}, u32[]{:S(2)}, u32[]{:S(2)}) collective-permute-start(f32[16,256]{1,0:T(8,128)S(1)} %add.314), channel_id=1, source_target_pairs={{0,4},{1,5},{2,6},{3,7},{4,0},{5,1},{6,2},{7,3},{8,12},{9,13},{10,... | collective-permute-start | bytes 49160 | tf_op jit(solution)/shard_map/ppermute | solution.py:18
  123.4 18.9 %collective-permute-start.30 = (f32[16,256]{1,0:T(8,128)S(1)}, f32[16,256]{1,0:T(8,128)S(1)}, u32[]{:S(2)}, u32[]{:S(2)}) collective-permute-start(f32[16,256]{1,0:T(8,128)S(1)} %add.281), channel_id=1, source_target_pairs={{0,4},{1,5},{2,6},{3,7},{4,0},{5,1},{6,2},{7,3},{8,12},{9,13},{10,... | collective-permute-start | bytes 49160 | tf_op jit(solution)/shard_map/ppermute | solution.py:18
  126.6 24.2 %collective-permute-start.18 = (f32[16,128]{1,0:T(8,128)S(1)}, f32[16,128]{1,0:T(8,128)S(1)}, u32[]{:S(2)}, u32[]{:S(2)}) collective-permute-start(f32[16,128]{1,0:T(8,128)S(1)} %add.271), channel_id=1, source_target_pairs={{0,8},{1,9},{2,10},{3,11},{4,12},{5,13},{6,14},{7,15},{8,0},{9,1},... | collective-permute-start | bytes 24584 | tf_op jit(solution)/shard_map/ppermute | solution.py:18
  133.9 20.1 %collective-permute-start.13 = (f32[16,128]{1,0:T(8,128)S(1)}, f32[16,128]{1,0:T(8,128)S(1)}, u32[]{:S(2)}, u32[]{:S(2)}) collective-permute-start(f32[16,128]{1,0:T(8,128)S(1)} %add.267), channel_id=1, source_target_pairs={{0,8},{1,9},{2,10},{3,11},{4,12},{5,13},{6,14},{7,15},{8,0},{9,1},... | collective-permute-start | bytes 24584 | tf_op jit(solution)/shard_map/ppermute | solution.py:18
  135.9 21.2 %collective-permute-start.82 = (f32[16,512]{1,0:T(8,128)S(1)}, f32[16,512]{1,0:T(8,128)S(1)}, u32[]{:S(2)}, u32[]{:S(2)}) collective-permute-start(f32[16,512]{1,0:T(8,128)S(1)} %slice_add_fusion.12), channel_id=1, source_target_pairs={{0,2},{1,3},{2,0},{3,1},{4,6},{5,7},{6,4},{7,5},{8,10},{9,11},{10,... | collective-permute-start | bytes 98312 | tf_op jit(solution)/shard_map/ppermute | solution.py:18
  142.3 21.0 %collective-permute-start.76 = (f32[16,256]{1,0:T(8,128)S(1)}, f32[16,256]{1,0:T(8,128)S(1)}, u32[]{:S(2)}, u32[]{:S(2)}) collective-permute-start(f32[16,256]{1,0:T(8,128)S(1)} %add.321), channel_id=1, source_target_pairs={{0,8},{1,9},{2,10},{3,11},{4,12},{5,13},{6,14},{7,15},{8,0},{9,1},... | collective-permute-start | bytes 49160 | tf_op jit(solution)/shard_map/ppermute | solution.py:18
  147.6 23.7 %collective-permute-start.64 = (f32[16,128]{1,0:T(8,128)S(1)}, f32[16,128]{1,0:T(8,128)S(1)}, u32[]{:S(2)}, u32[]{:S(2)}) collective-permute-start(f32[16,128]{1,0:T(8,128)S(1)} %add.311), channel_id=1, source_target_pairs={{0,16},{1,17},{2,18},{3,19},{4,20},{5,21},{6,22},{7,23},{8,24},{9,... | collective-permute-start | bytes 24584 | tf_op jit(solution)/shard_map/ppermute | solution.py:18
  150.8 17.6 %collective-permute-start.37 = (f32[16,512]{1,0:T(8,128)S(1)}, f32[16,512]{1,0:T(8,128)S(1)}, u32[]{:S(2)}, u32[]{:S(2)}) collective-permute-start(f32[16,512]{1,0:T(8,128)S(1)} %slice_add_fusion.13), channel_id=1, source_target_pairs={{0,2},{1,3},{2,0},{3,1},{4,6},{5,7},{6,4},{7,5},{8,10},{9,11},{10,... | collective-permute-start | bytes 98312 | tf_op jit(solution)/shard_map/ppermute | solution.py:18
  157.1 17.5 %collective-permute-start.31 = (f32[16,256]{1,0:T(8,128)S(1)}, f32[16,256]{1,0:T(8,128)S(1)}, u32[]{:S(2)}, u32[]{:S(2)}) collective-permute-start(f32[16,256]{1,0:T(8,128)S(1)} %add.282), channel_id=1, source_target_pairs={{0,8},{1,9},{2,10},{3,11},{4,12},{5,13},{6,14},{7,15},{8,0},{9,1},... | collective-permute-start | bytes 49160 | tf_op jit(solution)/shard_map/ppermute | solution.py:18
  166.4 23.3 %collective-permute-start.19 = (f32[16,128]{1,0:T(8,128)S(1)}, f32[16,128]{1,0:T(8,128)S(1)}, u32[]{:S(2)}, u32[]{:S(2)}) collective-permute-start(f32[16,128]{1,0:T(8,128)S(1)} %add.272), channel_id=1, source_target_pairs={{0,16},{1,17},{2,18},{3,19},{4,20},{5,21},{6,22},{7,23},{8,24},{9,... | collective-permute-start | bytes 24584 | tf_op jit(solution)/shard_map/ppermute | solution.py:18
  168.5 14.8 %collective-permute-start.83 = (f32[16,512]{1,0:T(8,128)S(1)}, f32[16,512]{1,0:T(8,128)S(1)}, u32[]{:S(2)}, u32[]{:S(2)}) collective-permute-start(f32[16,512]{1,0:T(8,128)S(1)} %add.327), channel_id=1, source_target_pairs={{0,4},{1,5},{2,6},{3,7},{4,0},{5,1},{6,2},{7,3},{8,12},{9,13},{10,... | collective-permute-start | bytes 98312 | tf_op jit(solution)/shard_map/ppermute | solution.py:18
  171.3 24.9 %collective-permute-start.77 = (f32[16,256]{1,0:T(8,128)S(1)}, f32[16,256]{1,0:T(8,128)S(1)}, u32[]{:S(2)}, u32[]{:S(2)}) collective-permute-start(f32[16,256]{1,0:T(8,128)S(1)} %add.322), channel_id=1, source_target_pairs={{0,16},{1,17},{2,18},{3,19},{4,20},{5,21},{6,22},{7,23},{8,24},{9,... | collective-permute-start | bytes 49160 | tf_op jit(solution)/shard_map/ppermute | solution.py:18
  180.1 18.9 %collective-permute-start.32 = (f32[16,256]{1,0:T(8,128)S(1)}, f32[16,256]{1,0:T(8,128)S(1)}, u32[]{:S(2)}, u32[]{:S(2)}) collective-permute-start(f32[16,256]{1,0:T(8,128)S(1)} %add.283), channel_id=1, source_target_pairs={{0,16},{1,17},{2,18},{3,19},{4,20},{5,21},{6,22},{7,23},{8,24},{9,... | collective-permute-start | bytes 49160 | tf_op jit(solution)/shard_map/ppermute | solution.py:18
  183.3 26.4 %collective-permute-start.25 = (f32[16,256]{1,0:T(8,128)S(1)}, f32[16,256]{1,0:T(8,128)S(1)}, u32[]{:S(2)}, u32[]{:S(2)}) collective-permute-start(f32[16,256]{1,0:T(8,128)S(1)} %add.277), channel_id=1, source_target_pairs={{0,16},{1,17},{2,18},{3,19},{4,20},{5,21},{6,22},{7,23},{8,24},{9,... | collective-permute-start | bytes 49160 | tf_op jit(solution)/shard_map/ppermute | solution.py:18
  185.4 33.8 %collective-permute-start.71 = (f32[16,256]{1,0:T(8,128)S(1)}, f32[16,256]{1,0:T(8,128)S(1)}, u32[]{:S(2)}, u32[]{:S(2)}) collective-permute-start(f32[16,256]{1,0:T(8,128)S(1)} %add.317), channel_id=1, source_target_pairs={{0,32},{1,33},{2,34},{3,35},{4,36},{5,37},{6,38},{7,39},{8,40},{9,... | collective-permute-start | bytes 49160 | tf_op jit(solution)/shard_map/ppermute | solution.py:18
  189.7 22.0 %collective-permute-start.84 = (f32[16,512]{1,0:T(8,128)S(1)}, f32[16,512]{1,0:T(8,128)S(1)}, u32[]{:S(2)}, u32[]{:S(2)}) collective-permute-start(f32[16,512]{1,0:T(8,128)S(1)} %add.328), channel_id=1, source_target_pairs={{0,8},{1,9},{2,10},{3,11},{4,12},{5,13},{6,14},{7,15},{8,0},{9,1},... | collective-permute-start | bytes 98312 | tf_op jit(solution)/shard_map/ppermute | solution.py:18
  196.2 19.8 %collective-permute-start.39 = (f32[16,512]{1,0:T(8,128)S(1)}, f32[16,512]{1,0:T(8,128)S(1)}, u32[]{:S(2)}, u32[]{:S(2)}) collective-permute-start(f32[16,512]{1,0:T(8,128)S(1)} %add.289), channel_id=1, source_target_pairs={{0,8},{1,9},{2,10},{3,11},{4,12},{5,13},{6,14},{7,15},{8,0},{9,1},... | collective-permute-start | bytes 98312 | tf_op jit(solution)/shard_map/ppermute | solution.py:18
  198.9 64.3 %collective-permute-start.45 = (bf16[16,64]{1,0:T(8,128)(2,1)S(1)}, bf16[16,64]{1,0:T(8,128)(2,1)S(1)}, u32[]{:S(2)}, u32[]{:S(2)}) collective-permute-start(bf16[16,64]{1,0:T(8,128)(2,1)S(1)} %slice.152), channel_id=1, source_target_pairs={{0,1},{1,0},{2,3},{3,2},{4,5},{5,4},{6,7},{7,6},{8,9},{9,8},{10,11... | collective-permute-start | bytes 6152 | tf_op jit(solution)/shard_map/ppermute | solution.py:18
  211.7 21.5 %collective-permute-start.26 = (f32[16,256]{1,0:T(8,128)S(1)}, f32[16,256]{1,0:T(8,128)S(1)}, u32[]{:S(2)}, u32[]{:S(2)}) collective-permute-start(f32[16,256]{1,0:T(8,128)S(1)} %add.278), channel_id=1, source_target_pairs={{0,32},{1,33},{2,34},{3,35},{4,36},{5,37},{6,38},{7,39},{8,40},{9,... | collective-permute-start | bytes 49160 | tf_op jit(solution)/shard_map/ppermute | solution.py:18
  221.3 15.7 %collective-permute-start.33 = (f32[16,256]{1,0:T(8,128)S(1)}, f32[16,256]{1,0:T(8,128)S(1)}, u32[]{:S(2)}, u32[]{:S(2)}) collective-permute-start(f32[16,256]{1,0:T(8,128)S(1)} %add.284), channel_id=1, source_target_pairs={{0,32},{1,33},{2,34},{3,35},{4,36},{5,37},{6,38},{7,39},{8,40},{9,... | collective-permute-start | bytes 49160 | tf_op jit(solution)/shard_map/ppermute | solution.py:18
  223.3 25.2 %collective-permute-start.79 = (f32[16,256]{1,0:T(8,128)S(1)}, f32[16,256]{1,0:T(8,128)S(1)}, u32[]{:S(2)}, u32[]{:S(2)}) collective-permute-start(f32[16,256]{1,0:T(8,128)S(1)} %add.324), channel_id=1, source_target_pairs={{0,64},{1,65},{2,66},{3,67},{4,68},{5,69},{6,70},{7,71},{8,72},{9,... | collective-permute-start | bytes 49160 | tf_op jit(solution)/shard_map/ppermute | solution.py:18
  237.0 29.2 %collective-permute-start.47 = (bf16[16,64]{1,0:T(8,128)(2,1)S(1)}, bf16[16,64]{1,0:T(8,128)(2,1)S(1)}, u32[]{:S(2)}, u32[]{:S(2)}) collective-permute-start(bf16[16,64]{1,0:T(8,128)(2,1)S(1)} %get-tuple-element.11), channel_id=1, source_target_pairs={{0,2},{1,3},{2,0},{3,1},{4,6},{5,7},{6,4},{7,5},{8,10},{9,11},{10,... | collective-permute-start | bytes 6152 | tf_op jit(solution)/shard_map/ppermute | solution.py:18
  239.3 14.0 %collective-permute-start.34 = (f32[16,256]{1,0:T(8,128)S(1)}, f32[16,256]{1,0:T(8,128)S(1)}, u32[]{:S(2)}, u32[]{:S(2)}) collective-permute-start(f32[16,256]{1,0:T(8,128)S(1)} %add.285), channel_id=1, source_target_pairs={{0,64},{1,65},{2,66},{3,67},{4,68},{5,69},{6,70},{7,71},{8,72},{9,... | collective-permute-start | bytes 49160 | tf_op jit(solution)/shard_map/ppermute | solution.py:18
  250.5 19.9 %collective-permute-start.50 = (bf16[16,64]{1,0:T(8,128)(2,1)S(1)}, bf16[16,64]{1,0:T(8,128)(2,1)S(1)}, u32[]{:S(2)}, u32[]{:S(2)}) collective-permute-start(bf16[16,64]{1,0:T(8,128)(2,1)S(1)} %add_convert_fusion.12), channel_id=1, source_target_pairs={{0,4},{1,5},{2,6},{3,7},{4,0},{5,1},{6,2},{7,3},{8,12},{9,13},{10,... | collective-permute-start | bytes 6152 | tf_op jit(solution)/shard_map/ppermute | solution.py:18
  253.2 22.0 %collective-permute-start.54 = (bf16[16,64]{1,0:T(8,128)(2,1)S(1)}, bf16[16,64]{1,0:T(8,128)(2,1)S(1)}, u32[]{:S(2)}, u32[]{:S(2)}) collective-permute-start(bf16[16,64]{1,0:T(8,128)(2,1)S(1)} %add_convert_fusion.11), channel_id=1, source_target_pairs={{0,8},{1,9},{2,10},{3,11},{4,12},{5,13},{6,14},{7,15},{8,0},{9,1},... | collective-permute-start | bytes 6152 | tf_op jit(solution)/shard_map/ppermute | solution.py:18
  260.0 17.4 %collective-permute-start.88 = (f32[16,512]{1,0:T(8,128)S(1)}, f32[16,512]{1,0:T(8,128)S(1)}, u32[]{:S(2)}, u32[]{:S(2)}) collective-permute-start(f32[16,512]{1,0:T(8,128)S(1)} %add.332), channel_id=1, source_target_pairs={{0,128},{1,129},{2,130},{3,131},{4,132},{5,133},{6,134},{7,135},{8... | collective-permute-start | bytes 98312 | tf_op jit(solution)/shard_map/ppermute | solution.py:18
  263.2 17.4 %collective-permute-start.59 = (bf16[16,128]{1,0:T(8,128)(2,1)S(1)}, bf16[16,128]{1,0:T(8,128)(2,1)S(1)}, u32[]{:S(2)}, u32[]{:S(2)}) collective-permute-start(bf16[16,128]{1,0:T(8,128)(2,1)S(1)} %add_convert_fusion.10), channel_id=1, source_target_pairs={{0,16},{1,17},{2,18},{3,19},{4,20},{5,21},{6,22},{7,23},{8,24},{9,... | collective-permute-start | bytes 12296 | tf_op jit(solution)/shard_map/ppermute | solution.py:18
  266.2 22.1 %collective-permute-start.65 = (bf16[16,128]{1,0:T(8,128)(2,1)S(1)}, bf16[16,128]{1,0:T(8,128)(2,1)S(1)}, u32[]{:S(2)}, u32[]{:S(2)}) collective-permute-start(bf16[16,128]{1,0:T(8,128)(2,1)S(1)} %add_convert_fusion.9), channel_id=1, source_target_pairs={{0,32},{1,33},{2,34},{3,35},{4,36},{5,37},{6,38},{7,39},{8,40},{9,... | collective-permute-start | bytes 12296 | tf_op jit(solution)/shard_map/ppermute | solution.py:18
  270.5 21.0 %collective-permute-start.72 = (bf16[16,256]{1,0:T(8,128)(2,1)S(1)}, bf16[16,256]{1,0:T(8,128)(2,1)S(1)}, u32[]{:S(2)}, u32[]{:S(2)}) collective-permute-start(bf16[16,256]{1,0:T(8,128)(2,1)S(1)} %add_convert_fusion.6), channel_id=1, source_target_pairs={{0,64},{1,65},{2,66},{3,67},{4,68},{5,69},{6,70},{7,71},{8,72},{9,... | collective-permute-start | bytes 24584 | tf_op jit(solution)/shard_map/ppermute | solution.py:18
  275.2 18.7 %collective-permute-start.80 = (bf16[16,256]{1,0:T(8,128)(2,1)S(1)}, bf16[16,256]{1,0:T(8,128)(2,1)S(1)}, u32[]{:S(2)}, u32[]{:S(2)}) collective-permute-start(bf16[16,256]{1,0:T(8,128)(2,1)S(1)} %add_convert_fusion.5), channel_id=1, source_target_pairs={{0,128},{1,129},{2,130},{3,131},{4,132},{5,133},{6,134},{7,135},{8... | collective-permute-start | bytes 24584 | tf_op jit(solution)/shard_map/ppermute | solution.py:18
  277.4 20.0 %collective-permute-start.43 = (f32[16,512]{1,0:T(8,128)S(1)}, f32[16,512]{1,0:T(8,128)S(1)}, u32[]{:S(2)}, u32[]{:S(2)}) collective-permute-start(f32[16,512]{1,0:T(8,128)S(1)} %add.293), channel_id=1, source_target_pairs={{0,128},{1,129},{2,130},{3,131},{4,132},{5,133},{6,134},{7,135},{8... | collective-permute-start | bytes 98312 | tf_op jit(solution)/shard_map/ppermute | solution.py:18
  280.6 26.0 %collective-permute-start = (bf16[16,64]{1,0:T(8,128)(2,1)S(1)}, bf16[16,64]{1,0:T(8,128)(2,1)S(1)}, u32[]{:S(2)}, u32[]{:S(2)}) collective-permute-start(bf16[16,64]{1,0:T(8,128)(2,1)S(1)} %slice.153), channel_id=1, source_target_pairs={{0,1},{1,0},{2,3},{3,2},{4,5},{5,4},{6,7},{7,6},{8,9},{9,8},{10,11... | collective-permute-start | bytes 6152 | tf_op jit(solution)/shard_map/ppermute | solution.py:18
  288.3 21.8 %collective-permute-start.2 = (bf16[16,64]{1,0:T(8,128)(2,1)S(1)}, bf16[16,64]{1,0:T(8,128)(2,1)S(1)}, u32[]{:S(2)}, u32[]{:S(2)}) collective-permute-start(bf16[16,64]{1,0:T(8,128)(2,1)S(1)} %get-tuple-element.25), channel_id=1, source_target_pairs={{0,2},{1,3},{2,0},{3,1},{4,6},{5,7},{6,4},{7,5},{8,10},{9,11},{10,... | collective-permute-start | bytes 6152 | tf_op jit(solution)/shard_map/ppermute | solution.py:18
  291.5 21.6 %collective-permute-start.5 = (bf16[16,64]{1,0:T(8,128)(2,1)S(1)}, bf16[16,64]{1,0:T(8,128)(2,1)S(1)}, u32[]{:S(2)}, u32[]{:S(2)}) collective-permute-start(bf16[16,64]{1,0:T(8,128)(2,1)S(1)} %add_convert_fusion.17), channel_id=1, source_target_pairs={{0,4},{1,5},{2,6},{3,7},{4,0},{5,1},{6,2},{7,3},{8,12},{9,13},{10,... | collective-permute-start | bytes 6152 | tf_op jit(solution)/shard_map/ppermute | solution.py:18
  294.0 21.3 %collective-permute-start.9 = (bf16[16,64]{1,0:T(8,128)(2,1)S(1)}, bf16[16,64]{1,0:T(8,128)(2,1)S(1)}, u32[]{:S(2)}, u32[]{:S(2)}) collective-permute-start(bf16[16,64]{1,0:T(8,128)(2,1)S(1)} %add_convert_fusion.16), channel_id=1, source_target_pairs={{0,8},{1,9},{2,10},{3,11},{4,12},{5,13},{6,14},{7,15},{8,0},{9,1},... | collective-permute-start | bytes 6152 | tf_op jit(solution)/shard_map/ppermute | solution.py:18
  303.5 17.3 %collective-permute-start.14 = (bf16[16,128]{1,0:T(8,128)(2,1)S(1)}, bf16[16,128]{1,0:T(8,128)(2,1)S(1)}, u32[]{:S(2)}, u32[]{:S(2)}) collective-permute-start(bf16[16,128]{1,0:T(8,128)(2,1)S(1)} %add_convert_fusion.15), channel_id=1, source_target_pairs={{0,16},{1,17},{2,18},{3,19},{4,20},{5,21},{6,22},{7,23},{8,24},{9,... | collective-permute-start | bytes 12296 | tf_op jit(solution)/shard_map/ppermute | solution.py:18
  306.6 14.2 %collective-permute-start.20 = (bf16[16,128]{1,0:T(8,128)(2,1)S(1)}, bf16[16,128]{1,0:T(8,128)(2,1)S(1)}, u32[]{:S(2)}, u32[]{:S(2)}) collective-permute-start(bf16[16,128]{1,0:T(8,128)(2,1)S(1)} %add_convert_fusion.14), channel_id=1, source_target_pairs={{0,32},{1,33},{2,34},{3,35},{4,36},{5,37},{6,38},{7,39},{8,40},{9,... | collective-permute-start | bytes 12296 | tf_op jit(solution)/shard_map/ppermute | solution.py:18
  (45 other events, 525.3 us)
where the time goes:
time: 328 us; the launch traced here: 323 us
  starting transfers between devices  306 us (93%)
  waiting for transfers between devices  6.05 us (2%)
  matrix products  5.33 us (2%)
    ppermute x90, starting transfers between devices, partner(): lax.ppermute(x, axis, [(i, i ^ 1 << apart) for i in range(lax.axis_size(a...  306 us
  transfers between devices with their start and end apart: 90, of which 4 were waited for; matrix products, arithmetic and copies ran while one was open for 1% of the time, Pallas kernels for 0%

commit v1 on v0

v1 whole, which is shorter than its diff:
```python
import jax
import jax.numpy as jnp
from jax import lax
from jax.experimental import pallas as pl
from jax.experimental.pallas import tpu as pltpu
from jax.sharding import PartitionSpec as P

MESH = pl.DeviceIdType.MESH
F32 = jnp.float32
BF16 = jnp.bfloat16

LEAF = 256
POINTS_HERE = 512
RANKS = 1600
LOW, MID, TOP7, TOP8 = 0, 320, 832, 1088

cell_units = 16.0
length_scale = 4.0
root_three = 1.7320508075688772
nugget = 0.1


def device(x, y, z, c):
    return ((x * 8 + y) * 8 + z) * 2 + c


def nt(a, b):
    return lax.dot_general(a, b, (((1,), (1,)), ((), ())), preferred_element_type=F32)


def nn(a, b):
    return jnp.dot(a, b, preferred_element_type=F32)


def send(src, dst, send_sem, recv_sem, to):
    pltpu.make_async_remote_copy(
        src_ref=src,
        dst_ref=dst,
        send_sem=send_sem,
        recv_sem=recv_sem,
        device_id=(to,),
        device_id_type=MESH,
    ).start()


def wait(ref, sem):
    pltpu.make_async_copy(ref, ref, sem).wait()


def matern(spots, leaf):
    cols = spots[:, leaf * LEAF : (leaf + 1) * LEAF]
    tall = jnp.transpose(cols)
    delta_x = tall[:, 0:1] - cols[0:1, :]
    delta_y = tall[:, 1:2] - cols[1:2, :]
    scaled = (root_three / length_scale) * jnp.sqrt(delta_x * delta_x + delta_y * delta_y)
    row = lax.broadcasted_iota(jnp.int32, (LEAF, LEAF), 0)
    col = lax.broadcasted_iota(jnp.int32, (LEAF, LEAF), 1)
    block = (1.0 + scaled) * jnp.exp(-scaled) + jnp.where(row == col, nugget, 0.0)
    return block.astype(BF16)


def kernel(
    coords_hbm, probes_hbm, u_hbm, v_hbm, f_ref, t_ref,
    coords, probes, signs, u, v,
    snd, low_snd, low0,
    r8, r7, r4, p8, p7, p4, q8, q7, q4, q1, q2, q3, fin,
    load, s1, s2, s3, sl, rs,
):
    me = lax.axis_index("pts")
    c = me % 2
    z = (me // 2) % 8
    y = (me // 16) % 8
    x = me // 128
    yc = y * 2 + c
    zc = z * 2 + c
    core0 = c == 0
    core1 = c == 1
    owner7 = jnp.logical_and(core1, y % 2 == 0)

    loads = [
        (probes_hbm, probes, None),
        (v_hbm, v, (TOP8, 512)),
        (u_hbm, u, (TOP8, 512)),
        (v_hbm, v, (TOP7, 256)),
        (u_hbm, u, (TOP7, 256)),
        (v_hbm, v, (MID, 512)),
        (u_hbm, u, (MID, 512)),
        (v_hbm, v, (LOW, 320)),
        (u_hbm, u, (LOW, 320)),
        (coords_hbm, coords, None),
    ]
    copies = []
    for i, (src, dst, rows) in enumerate(loads):
        if rows is not None:
            src, dst = src.at[pl.ds(*rows)], dst.at[pl.ds(*rows)]
        copies.append(pltpu.make_async_copy(src, dst, load.at[i]))
        copies[-1].start()

    barrier = pltpu.get_barrier_semaphore()

    def greet(to):
        pl.semaphore_signal(barrier, inc=1, device_id=(to,), device_id_type=MESH)

    @pl.loop(1, 16)
    def _(j):
        o = (yc + j) % 16
        greet(device(x, o // 2, z, o % 2))
        o = (zc + j) % 16
        greet(device(x, y, o // 2, o % 2))

    half = 2 - (x // 2) * 2
    beside = x + 1 - 2 * (x % 2)

    @pl.when(core0)
    def _():
        @pl.loop(0, 16)
        def _(j):
            greet(device(half + j // 8, y, j % 8, 0))

    @pl.when(core1)
    def _():
        @pl.loop(0, 8)
        def _(j):
            greet(device(beside, y, j, 1))

    copies[0].wait()
    signs[...] = (2 * probes[...] - 1).astype(BF16)

    copies[1].wait()
    part = nt(signs[...], v[pl.ds(TOP8, 512), :])
    for k in range(4):
        snd[k] = part[:, k * 128 : (k + 1) * 128]
    copies[2].wait()
    part = nt(signs[...], u[pl.ds(TOP8, 512), :])
    for k in range(4):
        snd[4 + k] = part[:, k * 128 : (k + 1) * 128]

    @pl.when(core0)
    def _():
        pl.semaphore_wait(barrier, 46)

    @pl.when(core1)
    def _():
        pl.semaphore_wait(barrier, 38)

    @pl.loop(1, 8)
    def _(j):
        k = (y + j) % 8
        send(snd.at[k], r8.at[yc], s1.at[0], rs.at[0], device(x, k, z, 0))

    @pl.when(core1)
    def _():
        send(snd.at[y], r8.at[yc], s1.at[1], rs.at[0], device(x, y, z, 0))

    @pl.when(core0)
    def _():
        r8[yc] = snd[y]

    copies[3].wait()
    part = nt(signs[...], v[pl.ds(TOP7, 256), :])
    for k in range(2):
        snd[8 + k] = part[:, k * 128 : (k + 1) * 128]
    copies[4].wait()
    part = nt(signs[...], u[pl.ds(TOP7, 256), :])
    for k in range(2):
        snd[10 + k] = part[:, k * 128 : (k + 1) * 128]

    @pl.loop(1, 4)
    def _(j):
        k = (y // 2 + j) % 4
        send(snd.at[8 + k], r7.at[yc], s1.at[2], rs.at[1], device(x, 2 * k, z, 1))

    @pl.when(jnp.logical_not(owner7))
    def _():
        k = y // 2
        send(snd.at[8 + k], r7.at[yc], s1.at[3], rs.at[1], device(x, 2 * k, z, 1))

    @pl.when(owner7)
    def _():
        r7[yc] = snd[8 + y // 2]

    copies[5].wait()
    part = nt(signs[...], v[pl.ds(MID, 512), :])
    for k, to in enumerate((0, 2, 4, 5)):
        snd[12 + to] = part[:, k * 128 : (k + 1) * 128]
    copies[6].wait()
    part = nt(signs[...], u[pl.ds(MID, 512), :])
    for k, to in enumerate((1, 3, 6, 7)):
        snd[12 + to] = part[:, k * 128 : (k + 1) * 128]

    @pl.loop(1, 8)
    def _(j):
        k = (z + j) % 8
        send(snd.at[12 + k], r4.at[zc], s1.at[4], rs.at[2], device(x, y, k, 1))

    @pl.when(core0)
    def _():
        send(snd.at[12 + z], r4.at[zc], s1.at[5], rs.at[2], device(x, y, z, 1))

    @pl.when(core1)
    def _():
        r4[zc] = snd[12 + z]

    copies[7].wait()
    low_f = nt(signs[...], v[pl.ds(64, 256), :])
    copies[8].wait()
    low_t = nt(signs[...], u[pl.ds(64, 256), :])
    joined = [
        jnp.concatenate([low_f[:, k * 64 : (k + 1) * 64], low_t[:, k * 64 : (k + 1) * 64]], axis=1)
        for k in range(4)
    ]
    low0[...] = joined[0].astype(BF16)
    for k in range(3):
        low_snd[k] = joined[k + 1]
    send(low0, fin.at[20], sl.at[0], rs.at[3], device(x, y, z, 1 - c))
    chip1 = z + 1 - 2 * (z % 2)
    send(low_snd.at[0], q1.at[c], sl.at[1], rs.at[4], device(x, y, chip1, 0))
    send(low_snd.at[0], q1.at[c], sl.at[2], rs.at[4], device(x, y, chip1, 1))
    pair = z // 2
    sib_pair = pair + 1 - 2 * (pair % 2)
    send(low_snd.at[1], q2.at[zc % 4], sl.at[3], rs.at[5], device(x, y, 2 * sib_pair + 1, 0))
    quad = z // 4
    send(low_snd.at[2], q3.at[zc % 8], sl.at[4], rs.at[6], device(x, y, 4 * (1 - quad) + 2, 0))

    @pl.when(core0)
    def _():
        wait(r8.at[pl.ds(0, 15)], rs.at[0])
        p8[...] = jnp.sum(r8[...], axis=0)

        @pl.loop(0, 16)
        def _(j):
            send(p8, q8.at[(x % 2) * 8 + z], s2.at[0], rs.at[7], device(half + j // 8, y, j % 8, 0))

    @pl.when(owner7)
    def _():
        wait(r7.at[pl.ds(0, 15)], rs.at[1])
        p7[...] = jnp.sum(r7[...], axis=0)

        @pl.loop(0, 8)
        def _(j):
            send(p7, q7.at[z], s2.at[1], rs.at[8], device(beside, y, j, 1))

    def mid_levels(action):
        for n, chosen in ((1, z < 2), (2, jnp.logical_and(z >= 2, z < 4)), (4, z >= 4)):
            @pl.when(jnp.logical_and(core1, chosen))
            def _():
                action(n)

    @pl.when(core1)
    def _():
        wait(r4.at[pl.ds(0, 15)], rs.at[2])
        p4[...] = jnp.sum(r4[...], axis=0)

    def mid_send(n):
        node = y // n
        first = (node + 1 - 2 * (node % 2)) * n
        for j in range(n):
            send(p4, q4.at[y % n], s2.at[2], rs.at[9], device(x, first + j, z, 1))

    mid_levels(mid_send)

    copies[9].wait()
    spots = coords[...].astype(F32) / cell_units
    for leaf in range(2):
        cols = pl.ds(leaf * LEAF, LEAF)
        other = pl.ds((1 - leaf) * LEAF, LEAF)
        near = nn(signs[:, cols], matern(spots, leaf))
        coef_f = nt(signs[:, other], v[pl.ds(0, 64), other]).astype(BF16)
        coef_t = nt(signs[:, other], u[pl.ds(0, 64), other]).astype(BF16)
        f_ref[:, cols] = near + nn(coef_f, u[pl.ds(0, 64), cols])
        t_ref[:, cols] = near + nn(coef_t, v[pl.ds(0, 64), cols])

    owner2 = jnp.logical_and(core0, z % 2 == 1)
    owner3 = jnp.logical_and(core0, z % 4 == 2)

    @pl.when(owner2)
    def _():
        wait(q2, rs.at[5])
        fin[22] = jnp.sum(q2[...], axis=0).astype(BF16)
        for j in range(1, 4):
            o = (zc % 4 + j) % 4
            send(fin.at[22], fin.at[22], s3.at[0], rs.at[10], device(x, y, 2 * pair + o // 2, o % 2))

    @pl.when(owner3)
    def _():
        wait(q3, rs.at[6])
        fin[23] = jnp.sum(q3[...], axis=0).astype(BF16)
        for j in range(1, 8):
            o = (zc % 8 + j) % 8
            send(fin.at[23], fin.at[23], s3.at[1], rs.at[11], device(x, y, 4 * quad + o // 2, o % 2))

    def mid_sum(n):
        wait(q4.at[pl.ds(0, n)], rs.at[9])
        fin[12 + z] = jnp.sum(q4[pl.ds(0, n)], axis=0).astype(BF16)

        @pl.loop(1, 16)
        def _(j):
            o = (zc + j) % 16
            send(fin.at[12 + z], fin.at[12 + z], s3.at[2], rs.at[12], device(x, y, o // 2, o % 2))

    mid_levels(mid_sum)

    @pl.when(core0)
    def _():
        wait(q8, rs.at[7])
        fin[y] = jnp.sum(q8[...], axis=0).astype(BF16)

        @pl.loop(1, 16)
        def _(j):
            o = (yc + j) % 16
            send(fin.at[y], fin.at[y], s3.at[3], rs.at[13], device(x, o // 2, z, o % 2))

    @pl.when(owner7)
    def _():
        wait(q7, rs.at[8])
        fin[8 + y // 2] = jnp.sum(q7[...], axis=0).astype(BF16)

        @pl.loop(1, 16)
        def _(j):
            o = (yc + j) % 16
            send(
                fin.at[8 + y // 2], fin.at[8 + y // 2], s3.at[4], rs.at[14], device(x, o // 2, z, o % 2)
            )

    wait(low0, rs.at[3])
    wait(q1, rs.at[4])
    fin[21] = jnp.sum(q1[...], axis=0).astype(BF16)

    @pl.when(jnp.logical_not(owner2))
    def _():
        wait(low0, rs.at[10])

    @pl.when(jnp.logical_not(owner3))
    def _():
        wait(low0, rs.at[11])

    low = [fin[20 + k] for k in range(4)]
    low_f = jnp.concatenate([part[:, :64] for part in low], axis=1)
    low_t = jnp.concatenate([part[:, 64:] for part in low], axis=1)
    f_ref[...] += nn(low_f, u[pl.ds(64, 256), :])
    t_ref[...] += nn(low_t, v[pl.ds(64, 256), :])

    @pl.when(core0)
    def _():
        wait(fin.at[pl.ds(0, 8)], rs.at[12])

    @pl.when(core1)
    def _():
        wait(fin.at[pl.ds(0, 7)], rs.at[12])

    def joint(chunks):
        return jnp.concatenate([fin[k] for k in chunks], axis=1)

    f_ref[...] += nn(joint((12, 14, 16, 17)), u[pl.ds(MID, 512), :])
    t_ref[...] += nn(joint((13, 15, 18, 19)), v[pl.ds(MID, 512), :])

    @pl.when(owner7)
    def _():
        wait(fin.at[pl.ds(0, 3)], rs.at[14])

    @pl.when(jnp.logical_not(owner7))
    def _():
        wait(fin.at[pl.ds(0, 4)], rs.at[14])

    @pl.when(core0)
    def _():
        wait(fin.at[pl.ds(0, 7)], rs.at[13])

    @pl.when(core1)
    def _():
        wait(fin.at[pl.ds(0, 8)], rs.at[13])

    f_ref[...] += nn(joint((8, 9, 0, 1, 2, 3)), u[pl.ds(TOP7, 768), :])
    t_ref[...] += nn(joint((10, 11, 4, 5, 6, 7)), v[pl.ds(TOP7, 768), :])

    wait(r8.at[pl.ds(0, 7)], s1.at[0])
    wait(r8.at[pl.ds(0, 3)], s1.at[2])
    wait(r8.at[pl.ds(0, 7)], s1.at[4])

    @pl.when(jnp.logical_not(owner7))
    def _():
        wait(p7, s1.at[3])

    wait(low0, sl.at[0])
    for k in range(1, 5):
        wait(p7, sl.at[k])

    @pl.when(core0)
    def _():
        wait(p4, s1.at[5])
        wait(q8, s2.at[0])
        wait(fin.at[pl.ds(0, 15)], s3.at[3])

    @pl.when(core1)
    def _():
        wait(p8, s1.at[1])
        wait(fin.at[pl.ds(0, 15)], s3.at[2])

    @pl.when(owner7)
    def _():
        wait(q7, s2.at[1])
        wait(fin.at[pl.ds(0, 15)], s3.at[4])

    mid_levels(lambda n: wait(q4.at[pl.ds(0, n)], s2.at[2]))

    @pl.when(owner2)
    def _():
        wait(fin.at[pl.ds(0, 3)], s3.at[0])

    @pl.when(owner3)
    def _():
        wait(fin.at[pl.ds(0, 7)], s3.at[1])


def shards(coords, probes, u_bases, v_bases):
    tile = (16, 128)
    return pl.pallas_call(
        kernel,
        out_shape=[jax.ShapeDtypeStruct((16, POINTS_HERE), F32)] * 2,
        in_specs=[pl.BlockSpec(memory_space=pl.ANY)] * 4,
        out_specs=[pl.BlockSpec(memory_space=pltpu.VMEM)] * 2,
        scratch_shapes=[
            pltpu.VMEM((2, POINTS_HERE), jnp.int32),
            pltpu.VMEM((16, POINTS_HERE), jnp.int32),
            pltpu.VMEM((16, POINTS_HERE), BF16),
            pltpu.VMEM((RANKS, POINTS_HERE), BF16),
            pltpu.VMEM((RANKS, POINTS_HERE), BF16),
            pltpu.VMEM((20,) + tile, F32),
            pltpu.VMEM((3,) + tile, F32),
            pltpu.VMEM(tile, BF16),
            pltpu.VMEM((16,) + tile, F32),
            pltpu.VMEM((16,) + tile, F32),
            pltpu.VMEM((16,) + tile, F32),
            pltpu.VMEM(tile, F32),
            pltpu.VMEM(tile, F32),
            pltpu.VMEM(tile, F32),
            pltpu.VMEM((16,) + tile, F32),
            pltpu.VMEM((8,) + tile, F32),
            pltpu.VMEM((4,) + tile, F32),
            pltpu.VMEM((2,) + tile, F32),
            pltpu.VMEM((4,) + tile, F32),
            pltpu.VMEM((8,) + tile, F32),
            pltpu.VMEM((24,) + tile, BF16),
            pltpu.SemaphoreType.DMA((10,)),
            pltpu.SemaphoreType.DMA((6,)),
            pltpu.SemaphoreType.DMA((3,)),
            pltpu.SemaphoreType.DMA((5,)),
            pltpu.SemaphoreType.DMA((5,)),
            pltpu.SemaphoreType.DMA((15,)),
        ],
        compiler_params=pltpu.CompilerParams(
            collective_id=0, has_side_effects=True, vmem_limit_bytes=60 * 1024 * 1024
        ),
    )(coords, probes, u_bases, v_bases)


def solution(mesh):
    return jax.shard_map(
        shards,
        mesh=mesh,
        in_specs=(P(None, "pts"), P(None, "pts"), P(None, "pts"), P(None, "pts")),
        out_specs=(P(None, "pts"), P(None, "pts")),
        check_vma=False,
    )
```

time: 328 us -> 37.1 us (0.11); the launches traced: 323 us -> 36.8 us
  starting transfers between devices: 306 us -> 0 us
  Pallas kernels: 0 us -> 33.4 us
  waiting for transfers between devices: 6.05 us -> 0 us
  matrix products: 5.33 us -> 0 us
    ppermute x90 -> x0, starting transfers between devices: 306 us -> none  [partner(): lax.ppermute(x, axis, [(i, i ^ 1 << apart) for i in range(lax.axis_size(a...]
    pallas_call x0 -> x1, Pallas kernels: none -> 33.4 us  [shards(): pl.pallas_call(kernel, out_shape=[jax.ShapeDtypeStruct((16, POINTS_HERE),...]
    ppermute x90 -> x0, waiting for transfers between devices: 6.05 us -> none  [partner(): lax.ppermute(x, axis, [(i, i ^ 1 << apart) for i in range(lax.axis_size(a...]
    dot_general x9 -> x0, matrix products: 5.33 us -> none  [the longest x1 1.91 us: shards(): lax.dot_general(sign_rows, cross_u, contract_dims, preferred_element_type...]
  transfers between devices with their start and end apart: 90 -> 0, of which waited for: 4 -> 0; matrix products, arithmetic and copies ran while one was open for 1% -> 0% of each run, Pallas kernels for 0% -> 0%
where the time goes in v1:
time: 37.1 us; the launch traced here: 36.8 us
  Pallas kernels  33.4 us (90%)
  local copies, waits for them, and re-layouts  2.75 us (7%)
  between operations  0.64 us (2%)
    pallas_call x1, Pallas kernels, shards(): pl.pallas_call(kernel, out_shape=[jax.ShapeDtypeStruct((16, POINTS_HERE),...  33.4 us
    unnamed x2, local copies, waits for them, and re-layouts  2.75 us

profile of v1, /device:TPU:1, one launch (start us, length us, event | category | flops | bytes accessed | tf_op | source)
XLA Modules:
  0.0 36.8 jit_solution(12858181481628101342)
XLA Ops:
  0.6 33.4 %shard_map.59 = (f32[16,512]{1,0:T(8,128)}, f32[16,512]{1,0:T(8,128)}) custom-call(s32[2,512]{1,0:T(2,128)} %coords_hbm.1, s32[16,512]{1,0:T(8,128)} %probes_hbm.1, bf16[1600,512]{1,0:T(8,128)(2,1)} %u_hbm.1, bf16[1600,512]{1,0:T(8,128)(2,1)} %v_hbm.1), custom_call_target="tpu_custom_call" | custom-call | tf_op jit(solution)/shard_map/pallas_call | solution.py:417
  34.1 1.4 %copy.8 = f32[16,512]{1,0:T(8,128)} copy(f32[16,512]{1,0:T(8,128)} %get-tuple-element.4) | data formatting | bytes 65536
  35.4 1.4 %copy.9 = f32[16,512]{1,0:T(8,128)} copy(f32[16,512]{1,0:T(8,128)} %get-tuple-element.5) | data formatting | bytes 65536

commit v2 on v1

v2 whole, which is shorter than its diff:
```python
import jax
import jax.numpy as jnp
from jax import lax
from jax.experimental import pallas as pl
from jax.experimental.pallas import tpu as pltpu
from jax.sharding import PartitionSpec as P

MESH = pl.DeviceIdType.MESH
F32 = jnp.float32
BF16 = jnp.bfloat16

LEAF = 256
VMEM_BYTES = 32 * 1024 * 1024
POINTS_HERE = 512
RANKS = 1600
LOW, MID, TOP7, TOP8 = 0, 320, 832, 1088

cell_units = 16.0
length_scale = 4.0
root_three = 1.7320508075688772
nugget = 0.1


def device(x, y, z, c):
    return ((x * 8 + y) * 8 + z) * 2 + c


def nt(a, b):
    return lax.dot_general(a, b, (((1,), (1,)), ((), ())), preferred_element_type=F32)


def nn(a, b):
    return jnp.dot(a, b, preferred_element_type=F32)


def send(src, dst, send_sem, recv_sem, to):
    pltpu.make_async_remote_copy(
        src_ref=src,
        dst_ref=dst,
        send_sem=send_sem,
        recv_sem=recv_sem,
        device_id=(to,),
        device_id_type=MESH,
    ).start()


def wait(ref, sem):
    pltpu.make_async_copy(ref, ref, sem).wait()


def total(ref, n):
    return sum(ref[k].astype(F32) for k in range(n))


def matern(spots, leaf):
    cols = spots[:, leaf * LEAF : (leaf + 1) * LEAF]
    tall = jnp.transpose(cols)
    delta_x = tall[:, 0:1] - cols[0:1, :]
    delta_y = tall[:, 1:2] - cols[1:2, :]
    scaled = (root_three / length_scale) * jnp.sqrt(delta_x * delta_x + delta_y * delta_y)
    row = lax.broadcasted_iota(jnp.int32, (LEAF, LEAF), 0)
    col = lax.broadcasted_iota(jnp.int32, (LEAF, LEAF), 1)
    block = (1.0 + scaled) * jnp.exp(-scaled) + jnp.where(row == col, nugget, 0.0)
    return block.astype(BF16)


def kernel(
    coords_hbm, probes_hbm, u_hbm, v_hbm, out_ref,
    coords, probes, signs, u, v,
    snd_y, snd_z, low_snd, low0,
    ry, rz, py, pz, qy, qz, q1, q2, q3, fin,
    load, s1, s2, s3, sl, rs, cross,
):
    me = lax.axis_index("pts")
    c = me % 2
    z = (me // 2) % 8
    y = (me // 16) % 8
    x = me // 128
    yc = y * 2 + c
    zc = z * 2 + c
    core0 = c == 0
    core1 = c == 1
    z_odd = z % 2 == 1
    owns_8f = jnp.logical_and(core0, y % 2 == 0)
    owns_7 = jnp.logical_and(core0, y % 2 == 1)
    owns_8t = jnp.logical_and(core1, z % 2 == 0)
    owns_45 = jnp.logical_and(core1, z_odd)
    owns_6 = jnp.logical_and(core0, z_odd)
    owns_z = jnp.logical_or(core1, z_odd)
    half = 2 - (x // 2) * 2
    beside = x + 1 - 2 * (x % 2)
    zslot = jnp.where(core1, z, 8 + z // 2)

    loads = [
        (probes_hbm, probes, None),
        (v_hbm, v, (TOP8, 512)),
        (u_hbm, u, (TOP8, 512)),
        (v_hbm, v, (TOP7, 256)),
        (u_hbm, u, (TOP7, 256)),
        (v_hbm, v, (MID, 512)),
        (u_hbm, u, (MID, 512)),
        (v_hbm, v, (LOW, 320)),
        (u_hbm, u, (LOW, 320)),
        (coords_hbm, coords, None),
    ]
    copies = []
    for i, (src, dst, rows) in enumerate(loads):
        if rows is not None:
            src, dst = src.at[pl.ds(*rows)], dst.at[pl.ds(*rows)]
        copies.append(pltpu.make_async_copy(src, dst, load.at[i]))
        copies[-1].start()

    barrier = pltpu.get_barrier_semaphore()

    def greet(to):
        pl.semaphore_signal(barrier, inc=1, device_id=(to,), device_id_type=MESH)

    for j in (4, 3, 5, 2, 6, 1, 7):
        for core in range(2):
            greet(device(x, (y + j) % 8, z, core))
            greet(device(x, y, (z + j) % 8, core))
    for j in (2, 1, 3):
        greet(device((x + j) % 4, y, z, c))
    greet(device(x, y, z, 1 - c))

    copies[0].wait()
    signs[...] = (2 * probes[...] - 1).astype(BF16)

    def keep(part, into, chunks):
        for k, to in enumerate(chunks):
            into[to] = part[:, k * 128 : (k + 1) * 128].astype(BF16)

    copies[1].wait()
    keep(nt(signs[...], v[pl.ds(TOP8, 512), :]), snd_y, (0, 2, 4, 6))
    copies[2].wait()
    keep(nt(signs[...], u[pl.ds(TOP8, 512), :]), snd_z, (0, 2, 4, 6))

    pl.semaphore_wait(barrier, 32)

    def to_y_owners(first, own):
        def one(k, sem):
            at = 2 * k + first
            send(snd_y.at[at], ry.at[yc], s1.at[sem], rs.at[0], device(x, at, z, 0))

        for j in (2, 1, 3):
            one((y // 2 + j) % 4, 0)

        @pl.when(jnp.logical_not(own))
        def _():
            one(y // 2, 1)

        @pl.when(own)
        def _():
            ry[yc] = snd_y[2 * (y // 2) + first]

    def to_z_owners(first, core, own):
        def slot(k):
            return 2 * k + first if core == 1 else 8 + k

        def one(k, sem):
            to = device(x, y, 2 * k + first, core)
            send(snd_z.at[slot(k)], rz.at[zc], s1.at[sem], rs.at[1], to)

        for j in (2, 1, 3):
            one((z // 2 + j) % 4, 0)

        @pl.when(jnp.logical_not(own))
        def _():
            one(z // 2, 1)

        @pl.when(own)
        def _():
            rz[zc] = snd_z[slot(z // 2)]

    to_y_owners(0, owns_8f)
    to_z_owners(0, 1, owns_8t)
    for j in (2, 1, 3):
        pl.semaphore_signal(
            cross, inc=1, device_id=(device((x + j) % 4, y, z, c),), device_id_type=MESH
        )

    copies[3].wait()
    keep(nt(signs[...], v[pl.ds(TOP7, 256), :]), snd_y, (1, 3))
    copies[4].wait()
    keep(nt(signs[...], u[pl.ds(TOP7, 256), :]), snd_y, (5, 7))

    to_y_owners(1, owns_7)

    copies[5].wait()
    keep(nt(signs[...], v[pl.ds(MID, 512), :]), snd_z, (1, 5, 8, 9))
    copies[6].wait()
    keep(nt(signs[...], u[pl.ds(MID, 512), :]), snd_z, (3, 7, 10, 11))

    to_z_owners(1, 1, owns_45)
    to_z_owners(1, 0, owns_6)

    copies[7].wait()
    low_f = nt(signs[...], v[pl.ds(64, 256), :])
    copies[8].wait()
    low_t = nt(signs[...], u[pl.ds(64, 256), :])
    joined = [
        jnp.concatenate([low_f[:, k * 64 : (k + 1) * 64], low_t[:, k * 64 : (k + 1) * 64]], axis=1)
        for k in range(4)
    ]
    low0[...] = joined[0].astype(BF16)
    for k in range(3):
        low_snd[k] = joined[k + 1]
    send(low0, fin.at[20], sl.at[0], rs.at[3], device(x, y, z, 1 - c))
    chip1 = z + 1 - 2 * (z % 2)
    send(low_snd.at[0], q1.at[c], sl.at[1], rs.at[4], device(x, y, chip1, 0))
    send(low_snd.at[0], q1.at[c], sl.at[2], rs.at[4], device(x, y, chip1, 1))
    pair = z // 2
    sib_pair = pair + 1 - 2 * (pair % 2)
    send(low_snd.at[1], q2.at[zc % 4], sl.at[3], rs.at[5], device(x, y, 2 * sib_pair, 0))
    quad = z // 4
    send(low_snd.at[2], q3.at[zc % 8], sl.at[4], rs.at[6], device(x, y, 4 * (1 - quad) + 2, 0))

    @pl.when(core0)
    def _():
        wait(ry.at[pl.ds(0, 15)], rs.at[0])
        py[...] = total(ry, 16).astype(BF16)

    pl.semaphore_wait(cross, 3)

    @pl.when(owns_8f)
    def _():
        for j in (4, 3, 5, 2, 6, 1, 7, 0):
            for h in range(2):
                to = device(half + h, y, (z + j) % 8, 0)
                send(py, qy.at[(x % 2) * 8 + z], s2.at[0], rs.at[2], to)

    @pl.when(owns_7)
    def _():
        for j in (4, 3, 5, 2, 6, 1, 7, 0):
            send(py, qy.at[z], s2.at[0], rs.at[2], device(beside, y, (z + j) % 8, 0))

    @pl.when(owns_z)
    def _():
        wait(rz.at[pl.ds(0, 15)], rs.at[1])
        pz[...] = total(rz, 16).astype(BF16)

    @pl.when(owns_8t)
    def _():
        for j in (4, 3, 5, 2, 6, 1, 7, 0):
            for h in range(2):
                to = device(half + h, (y + j) % 8, z, 1)
                send(pz, qz.at[(x % 2) * 8 + y], s2.at[1], rs.at[7], to)

    def mid_levels(action):
        for n, chosen in (
            (1, jnp.logical_and(owns_45, z < 4)),
            (2, jnp.logical_and(owns_45, z >= 4)),
            (4, owns_6),
        ):
            @pl.when(chosen)
            def _():
                action(n)

    def mid_send(n):
        node = y // n
        first = (node + 1 - 2 * (node % 2)) * n
        for j in range(n):
            send(pz, qz.at[y % n], s2.at[1], rs.at[7], device(x, first + j, z, c))

    mid_levels(mid_send)

    copies[9].wait()
    spots = coords[...].astype(F32) / cell_units
    for leaf in range(2):
        cols = pl.ds(leaf * LEAF, LEAF)
        other = pl.ds((1 - leaf) * LEAF, LEAF)
        near = nn(signs[:, cols], matern(spots, leaf))
        coef_f = nt(signs[:, other], v[pl.ds(0, 64), other]).astype(BF16)
        coef_t = nt(signs[:, other], u[pl.ds(0, 64), other]).astype(BF16)
        out_ref[:16, cols] = near + nn(coef_f, u[pl.ds(0, 64), cols])
        out_ref[16:, cols] = near + nn(coef_t, v[pl.ds(0, 64), cols])

    owner2 = jnp.logical_and(core0, z % 2 == 0)
    owner3 = jnp.logical_and(core0, z % 4 == 2)

    @pl.when(owner2)
    def _():
        wait(q2, rs.at[5])
        fin[22] = total(q2, 4).astype(BF16)
        for j in range(1, 4):
            o = (zc % 4 + j) % 4
            send(fin.at[22], fin.at[22], s3.at[0], rs.at[8], device(x, y, 2 * pair + o // 2, o % 2))

    @pl.when(owner3)
    def _():
        wait(q3, rs.at[6])
        fin[23] = total(q3, 8).astype(BF16)
        for j in range(1, 8):
            o = (zc % 8 + j) % 8
            send(fin.at[23], fin.at[23], s3.at[1], rs.at[9], device(x, y, 4 * quad + o // 2, o % 2))

    def to_z_group(sem):
        for j in (4, 3, 5, 2, 6, 1, 7):
            for core in range(2):
                to = device(x, y, (z + j) % 8, core)
                send(fin.at[8 + zslot], fin.at[8 + zslot], s3.at[2], rs.at[sem], to)
        send(fin.at[8 + zslot], fin.at[8 + zslot], s3.at[2], rs.at[sem], device(x, y, z, 1 - c))

    def to_y_group(sem):
        for j in (4, 3, 5, 2, 6, 1, 7):
            for core in range(2):
                send(fin.at[y], fin.at[y], s3.at[3], rs.at[sem], device(x, (y + j) % 8, z, core))
        send(fin.at[y], fin.at[y], s3.at[3], rs.at[sem], device(x, y, z, 1))

    def mid_sum(n):
        wait(qz.at[pl.ds(0, n)], rs.at[7])
        fin[8 + zslot] = total(qz, n).astype(BF16)
        to_z_group(10)

    mid_levels(mid_sum)

    @pl.when(owns_7)
    def _():
        wait(qy.at[pl.ds(0, 8)], rs.at[2])
        fin[y] = total(qy, 8).astype(BF16)
        to_y_group(11)

    @pl.when(owns_8f)
    def _():
        wait(qy, rs.at[2])
        fin[y] = total(qy, 16).astype(BF16)
        to_y_group(12)

    @pl.when(owns_8t)
    def _():
        wait(qz, rs.at[7])
        fin[8 + zslot] = total(qz, 16).astype(BF16)
        to_z_group(13)

    wait(low0, rs.at[3])
    wait(q1, rs.at[4])
    fin[21] = total(q1, 2).astype(BF16)

    @pl.when(jnp.logical_not(owner2))
    def _():
        wait(low0, rs.at[8])

    @pl.when(jnp.logical_not(owner3))
    def _():
        wait(low0, rs.at[9])

    low = [fin[20 + k] for k in range(4)]
    low_f = jnp.concatenate([part[:, :64] for part in low], axis=1)
    low_t = jnp.concatenate([part[:, 64:] for part in low], axis=1)
    out_ref[:16, :] += nn(low_f, u[pl.ds(64, 256), :])
    out_ref[16:, :] += nn(low_t, v[pl.ds(64, 256), :])

    def await_chunks(n, sem, own):
        @pl.when(own)
        def _():
            wait(fin.at[pl.ds(0, n - 1)], rs.at[sem])

        @pl.when(jnp.logical_not(own))
        def _():
            wait(fin.at[pl.ds(0, n)], rs.at[sem])

    await_chunks(8, 10, z_odd)

    def joint(chunks):
        return jnp.concatenate([fin[k] for k in chunks], axis=1)

    out_ref[:16, :] += nn(joint((9, 13, 16, 17)), u[pl.ds(MID, 512), :])
    out_ref[16:, :] += nn(joint((11, 15, 18, 19)), v[pl.ds(MID, 512), :])

    await_chunks(4, 11, owns_7)

    out_ref[:16, :] += nn(joint((1, 3)), u[pl.ds(TOP7, 256), :])
    out_ref[16:, :] += nn(joint((5, 7)), v[pl.ds(TOP7, 256), :])

    await_chunks(4, 12, owns_8f)
    await_chunks(4, 13, owns_8t)

    out_ref[:16, :] += nn(joint((0, 2, 4, 6)), u[pl.ds(TOP8, 512), :])
    out_ref[16:, :] += nn(joint((8, 10, 12, 14)), v[pl.ds(TOP8, 512), :])

    wait(ry.at[pl.ds(0, 15)], s1.at[0])

    @pl.when(owns_6)
    def _():
        wait(ry.at[pl.ds(0, 3)], s1.at[1])

    @pl.when(jnp.logical_not(owns_6))
    def _():
        wait(ry.at[pl.ds(0, 4)], s1.at[1])

    wait(low0, sl.at[0])
    for k in range(1, 5):
        wait(low_snd.at[0], sl.at[k])

    @pl.when(owns_8f)
    def _():
        wait(qy, s2.at[0])

    @pl.when(owns_7)
    def _():
        wait(qy.at[pl.ds(0, 8)], s2.at[0])

    @pl.when(owns_8t)
    def _():
        wait(qz, s2.at[1])

    mid_levels(lambda n: wait(qz.at[pl.ds(0, n)], s2.at[1]))

    @pl.when(core0)
    def _():
        wait(fin.at[pl.ds(0, 15)], s3.at[3])

    @pl.when(owns_z)
    def _():
        wait(fin.at[pl.ds(0, 15)], s3.at[2])

    @pl.when(owner2)
    def _():
        wait(fin.at[pl.ds(0, 3)], s3.at[0])

    @pl.when(owner3)
    def _():
        wait(fin.at[pl.ds(0, 7)], s3.at[1])


def shards(coords, probes, u_bases, v_bases):
    tile = (16, 128)
    operands = [
        pltpu.with_memory_space_constraint(a, pltpu.HBM) for a in (coords, probes, u_bases, v_bases)
    ]
    both = pl.pallas_call(
        kernel,
        out_shape=jax.ShapeDtypeStruct((32, POINTS_HERE), F32),
        in_specs=[pl.BlockSpec(memory_space=pl.ANY)] * 4,
        out_specs=pl.BlockSpec(memory_space=pltpu.VMEM),
        scratch_shapes=[
            pltpu.VMEM((2, POINTS_HERE), jnp.int32),
            pltpu.VMEM((16, POINTS_HERE), jnp.int32),
            pltpu.VMEM((16, POINTS_HERE), BF16),
            pltpu.VMEM((RANKS, POINTS_HERE), BF16),
            pltpu.VMEM((RANKS, POINTS_HERE), BF16),
            pltpu.VMEM((8,) + tile, BF16),
            pltpu.VMEM((12,) + tile, BF16),
            pltpu.VMEM((3,) + tile, F32),
            pltpu.VMEM(tile, BF16),
            pltpu.VMEM((16,) + tile, BF16),
            pltpu.VMEM((16,) + tile, BF16),
            pltpu.VMEM(tile, BF16),
            pltpu.VMEM(tile, BF16),
            pltpu.VMEM((16,) + tile, BF16),
            pltpu.VMEM((16,) + tile, BF16),
            pltpu.VMEM((2,) + tile, F32),
            pltpu.VMEM((4,) + tile, F32),
            pltpu.VMEM((8,) + tile, F32),
            pltpu.VMEM((24,) + tile, BF16),
            pltpu.SemaphoreType.DMA((10,)),
            pltpu.SemaphoreType.DMA((2,)),
            pltpu.SemaphoreType.DMA((2,)),
            pltpu.SemaphoreType.DMA((4,)),
            pltpu.SemaphoreType.DMA((5,)),
            pltpu.SemaphoreType.DMA((14,)),
            pltpu.SemaphoreType.REGULAR,
        ],
        compiler_params=pltpu.CompilerParams(
            collective_id=0, has_side_effects=True, vmem_limit_bytes=VMEM_BYTES
        ),
    )(*operands)
    return both[:16], both[16:]


def solution(mesh):
    return jax.shard_map(
        shards,
        mesh=mesh,
        in_specs=(P(None, "pts"), P(None, "pts"), P(None, "pts"), P(None, "pts")),
        out_specs=(P(None, "pts"), P(None, "pts")),
        check_vma=False,
    )
```

time: 37.1 us -> 32.6 us (0.88)
  Pallas kernels: 33.4 us -> 31.2 us
  local copies, waits for them, and re-layouts: 2.75 us -> 0.63 us
    unnamed x2 -> x0, local copies, waits for them, and re-layouts: 2.75 us -> none
    pallas_call x1, Pallas kernels: 33.4 us -> 31.2 us  [shards(): pl.pallas_call(kernel, out_shape=jax.ShapeDtypeStruct((32, POINTS_HERE),...]
    slice x0 -> x1, local copies, waits for them, and re-layouts: none -> 0.63 us  [shards(): return (both[:16], both[16:])]
where the time goes in v2:
time: 32.6 us; the launch traced here: 32.5 us
  Pallas kernels  31.2 us (96%)
  between operations  0.64 us (2%)
  local copies, waits for them, and re-layouts  0.63 us (2%)
    pallas_call x1, Pallas kernels, shards(): pl.pallas_call(kernel, out_shape=jax.ShapeDtypeStruct((32, POINTS_HERE),...  31.2 us

profile of v2, /device:TPU:1, one launch (start us, length us, event | category | flops | bytes accessed | tf_op | source)
XLA Modules:
  0.0 32.5 jit_solution(18399818714525521946)
XLA Ops:
  0.6 31.2 %shard_map.59 = f32[32,512]{1,0:T(8,128)S(1)} custom-call(s32[2,512]{1,0:T(2,128)} %coords_hbm.1, s32[16,512]{1,0:T(8,128)} %probes_hbm.1, bf16[1600,512]{1,0:T(8,128)(2,1)} %u_hbm.1, bf16[1600,512]{1,0:T(8,128)(2,1)} %v_hbm.1), custom_call_target="tpu_custom_call" | custom-call | tf_op jit(solution)/shard_map/pallas_call | solution.py:431
  31.9 0.6 %fusion = (f32[16,512]{1,0:T(8,128)}, f32[16,512]{1,0:T(8,128)}) fusion(f32[32,512]{1,0:T(8,128)S(1)} %shard_map.59), kind=kLoop, calls=%fused_computation | loop fusion | bytes 131072 | tf_op jit(solution)/shard_map/slice | solution.py:468

commit v3 on v0

v3 whole, which is shorter than its diff:
```python
import jax
import jax.numpy as jnp
from jax import lax
from jax.experimental import pallas as pl
from jax.experimental.pallas import tpu as pltpu
from jax.sharding import PartitionSpec as P

MESH = pl.DeviceIdType.MESH
F32 = jnp.float32
BF16 = jnp.bfloat16

LEAF = 256
VMEM_BYTES = 32 * 1024 * 1024
POINTS_HERE = 512
RANKS = 1600
LOW, MID, TOP7, TOP8 = 0, 320, 832, 1088

cell_units = 16.0
length_scale = 4.0
root_three = 1.7320508075688772
nugget = 0.1


def device(x, y, z, c):
    return ((x * 8 + y) * 8 + z) * 2 + c


def nt(a, b):
    return lax.dot_general(a, b, (((1,), (1,)), ((), ())), preferred_element_type=F32)


def nn(a, b):
    return jnp.dot(a, b, preferred_element_type=F32)


def send(src, dst, send_sem, recv_sem, to):
    pltpu.make_async_remote_copy(
        src_ref=src,
        dst_ref=dst,
        send_sem=send_sem,
        recv_sem=recv_sem,
        device_id=(to,),
        device_id_type=MESH,
    ).start()


def wait(ref, sem):
    pltpu.make_async_copy(ref, ref, sem).wait()


def matern(spots, leaf):
    cols = spots[:, leaf * LEAF : (leaf + 1) * LEAF]
    tall = jnp.transpose(cols)
    delta_x = tall[:, 0:1] - cols[0:1, :]
    delta_y = tall[:, 1:2] - cols[1:2, :]
    scaled = (root_three / length_scale) * jnp.sqrt(delta_x * delta_x + delta_y * delta_y)
    row = lax.broadcasted_iota(jnp.int32, (LEAF, LEAF), 0)
    col = lax.broadcasted_iota(jnp.int32, (LEAF, LEAF), 1)
    block = (1.0 + scaled) * jnp.exp(-scaled) + jnp.where(row == col, nugget, 0.0)
    return block.astype(BF16)


def kernel(
    coords_hbm, probes_hbm, u_hbm, v_hbm, out_ref,
    coords, probes, signs, u, v,
    snd, low0, got, mine, q8, q7, qm, low_out, fin, fin0,
    load, s1, s2, s3, sl, rs,
):
    me = lax.axis_index("pts")
    c = me % 2
    z = (me // 2) % 8
    y = (me // 16) % 8
    x = me // 128
    zc = z * 2 + c
    owns = zc < 8
    owns_8 = zc < 4
    owns_47 = jnp.logical_and(zc >= 4, zc < 8)
    half = 2 - (x // 2) * 2
    beside = x + 1 - 2 * (x % 2)

    def member(place):
        return device(x, y, place // 2, place % 2)

    loads = [
        (probes_hbm, probes, None),
        (v_hbm, v, (TOP8, 512)),
        (u_hbm, u, (TOP8, 512)),
        (v_hbm, v, (MID, 512)),
        (u_hbm, u, (MID, 512)),
        (v_hbm, v, (TOP7, 256)),
        (u_hbm, u, (TOP7, 256)),
        (v_hbm, v, (LOW, 320)),
        (u_hbm, u, (LOW, 320)),
        (coords_hbm, coords, None),
    ]
    copies = []
    for i, (src, dst, rows) in enumerate(loads):
        if rows is not None:
            src, dst = src.at[pl.ds(*rows)], dst.at[pl.ds(*rows)]
        copies.append(pltpu.make_async_copy(src, dst, load.at[i]))
        copies[-1].start()

    barrier = pltpu.get_barrier_semaphore()

    def greet(to):
        pl.semaphore_signal(barrier, inc=1, device_id=(to,), device_id_type=MESH)

    @pl.when(owns)
    def _():
        for j in range(1, 16):
            greet(member((zc + j) % 16))

    @pl.when(jnp.logical_not(owns))
    def _():
        greet(device(x, y, z, 1 - c))

    @pl.when(owns_8)
    def _():
        for h in range(2):
            for j in range(8):
                greet(device(half + h, j, z, c))

    @pl.when(owns_47)
    def _():
        for j in range(8):
            greet(device(beside, j, z, c))
        for j in range(1, 8):
            greet(device(x, (y + j) % 8, z, c))

    copies[0].wait()
    signs[...] = (2 * probes[...] - 1).astype(BF16)

    def keep(part, places):
        for k, (owner, row) in enumerate(places):
            snd[owner, row] = part[:, k * 128 : (k + 1) * 128].astype(BF16)

    def to_owners(first, rows):
        def one(place, sem):
            send(snd.at[place, rows], got.at[zc, rows], s1.at[sem], rs.at[0], member(place))

        for j in range(1, 4):
            one(first + (zc + j) % 4, 0)

        own = jnp.logical_and(zc >= first, zc < first + 4)

        @pl.when(jnp.logical_not(own))
        def _():
            one(first + zc % 4, 1)

        @pl.when(own)
        def _():
            got[zc, rows] = snd[zc, rows]

    copies[1].wait()
    keep(nt(signs[...], v[pl.ds(TOP8, 512), :]), [(k, 0) for k in range(4)])

    @pl.when(owns_8)
    def _():
        pl.semaphore_wait(barrier, 23)

    @pl.when(owns_47)
    def _():
        pl.semaphore_wait(barrier, 22)

    @pl.when(jnp.logical_not(owns))
    def _():
        pl.semaphore_wait(barrier, 9)

    to_owners(0, pl.ds(0, 1))

    copies[2].wait()
    keep(nt(signs[...], u[pl.ds(TOP8, 512), :]), [(k, 1) for k in range(4)])

    to_owners(0, pl.ds(1, 1))

    copies[3].wait()
    keep(nt(signs[...], v[pl.ds(MID, 512), :]), [(4, 1), (5, 1), (6, 1), (6, 2)])
    copies[4].wait()
    keep(nt(signs[...], u[pl.ds(MID, 512), :]), [(4, 2), (5, 2), (7, 1), (7, 2)])

    copies[5].wait()
    keep(nt(signs[...], v[pl.ds(TOP7, 256), :]), [(4, 0), (5, 0)])
    copies[6].wait()
    keep(nt(signs[...], u[pl.ds(TOP7, 256), :]), [(6, 0), (7, 0)])

    to_owners(4, pl.ds(0, 3))

    copies[7].wait()
    low_f = nt(signs[...], v[pl.ds(64, 256), :])
    copies[8].wait()
    low_t = nt(signs[...], u[pl.ds(64, 256), :])
    joined = [
        jnp.concatenate(
            [low_f[:, k * 64 : (k + 1) * 64], low_t[:, k * 64 : (k + 1) * 64]], axis=1
        ).astype(BF16)
        for k in range(4)
    ]
    low0[...] = joined[0]
    send(low0, fin0, sl, rs.at[2], device(x, y, z, 1 - c))
    for owner in range(3):
        snd[owner, 2] = joined[3 - owner]

        @pl.when(zc == owner)
        def _():
            got[zc, 2] = snd[owner, 2]

        @pl.when(zc != owner)
        def _():
            send(snd.at[owner, 2], got.at[zc, 2], s1.at[2], rs.at[1], member(owner))

    copies[9].wait()
    spots = coords[...].astype(F32) / cell_units
    for leaf in range(2):
        cols = pl.ds(leaf * LEAF, LEAF)
        other = pl.ds((1 - leaf) * LEAF, LEAF)
        near = nn(signs[:, cols], matern(spots, leaf))
        coef_f = nt(signs[:, other], v[pl.ds(0, 64), other]).astype(BF16)
        coef_t = nt(signs[:, other], u[pl.ds(0, 64), other]).astype(BF16)
        out_ref[:16, cols] = near + nn(coef_f, u[pl.ds(0, 64), cols])
        out_ref[16:, cols] = near + nn(coef_t, v[pl.ds(0, 64), cols])

    def total(parts):
        return sum(part.astype(F32) for part in parts).astype(BF16)

    @pl.when(owns_8)
    def _():
        wait(got.at[pl.ds(0, 10)], rs.at[0])
        for a in range(2):
            mine[a] = total(got[k, a] for k in range(16))

    @pl.when(owns_47)
    def _():
        wait(got.at[pl.ds(0, 15)], rs.at[0])
        for a in range(3):
            mine[a] = total(got[k, a] for k in range(16))

    @pl.when(owns_8)
    def _():
        for j in (0, 1, 7, 2, 6, 3, 5, 4):
            for h in range(2):
                to = device(half + h, j, z, c)
                send(mine.at[pl.ds(0, 2)], q8.at[(x % 2) * 8 + y], s2.at[0], rs.at[3], to)

    @pl.when(owns_47)
    def _():
        for j in (0, 1, 7, 2, 6, 3, 5, 4):
            send(mine.at[0], q7.at[y], s2.at[1], rs.at[4], device(beside, j, z, c))

    def mid_levels(action):
        for n, chosen in ((1, zc == 4), (2, zc == 5), (4, jnp.logical_and(zc >= 6, zc < 8))):
            @pl.when(chosen)
            def _():
                action(n)

    def mid_send(n):
        node = y // n
        first = (node + 1 - 2 * (node % 2)) * n
        for j in range(n):
            send(
                mine.at[pl.ds(1, 2)], qm.at[y % n], s2.at[2], rs.at[5], device(x, first + j, z, c)
            )

    mid_levels(mid_send)

    for owner, size in ((0, 8), (1, 4), (2, 2)):
        @pl.when(zc == owner)
        def _():
            wait(got.at[pl.ds(0, 5)], rs.at[1])
            groups = 16 // size
            for g in range(groups):
                sib = g ^ 1
                low_out[g] = total(got[k, 2] for k in range(sib * size, (sib + 1) * size))
            fin[owner, 2] = low_out[owner // size]
            for place in range(16):
                if place != owner:
                    send(
                        low_out.at[place // size], fin.at[owner, 2], s3.at[0], rs.at[6 + owner],
                        member(place),
                    )

    def hand_out(rows, send_sem, recv_sem, first):
        def one(place):
            send(fin.at[zc, rows], fin.at[zc, rows], s3.at[send_sem], rs.at[recv_sem], member(place))

        for place in range(first):
            one(place)
        for j in range(1, 4):
            one(first + (zc + j) % 4)
        for place in range(first + 4, 16):
            one(place)

    def mid_sum(n):
        wait(qm.at[pl.ds(0, n)], rs.at[5])
        for a in range(2):
            fin[zc, 1 + a] = total(qm[k, a] for k in range(n))
        hand_out(pl.ds(1, 2), 1, 9, 4)

    mid_levels(mid_sum)

    @pl.when(owns_47)
    def _():
        wait(q7, rs.at[4])
        fin[zc, 0] = total(q7[k] for k in range(8))
        hand_out(pl.ds(0, 1), 2, 10, 4)

    @pl.when(owns_8)
    def _():
        wait(q8, rs.at[3])
        for a in range(2):
            fin[zc, a] = total(q8[k, a] for k in range(16))
        hand_out(pl.ds(0, 2), 3, 11, 0)

    wait(low0, rs.at[2])
    for owner in range(3):
        @pl.when(zc != owner)
        def _():
            wait(low0, rs.at[6 + owner])

    low = [fin0[...]] + [fin[owner, 2] for owner in (2, 1, 0)]
    low_f = jnp.concatenate([part[:, :64] for part in low], axis=1)
    low_t = jnp.concatenate([part[:, 64:] for part in low], axis=1)
    out_ref[:16, :] += nn(low_f, u[pl.ds(64, 256), :])
    out_ref[16:, :] += nn(low_t, v[pl.ds(64, 256), :])

    def await_chunks(ref, n, sem, own):
        @pl.when(own)
        def _():
            wait(ref.at[pl.ds(0, n - n // 4)], rs.at[sem])

        @pl.when(jnp.logical_not(own))
        def _():
            wait(ref.at[pl.ds(0, n)], rs.at[sem])

    await_chunks(qm, 4, 9, owns_47)

    def joint(places):
        return jnp.concatenate([fin[owner, row] for owner, row in places], axis=1)

    out_ref[:16, :] += nn(joint([(4, 1), (5, 1), (6, 1), (6, 2)]), u[pl.ds(MID, 512), :])
    out_ref[16:, :] += nn(joint([(4, 2), (5, 2), (7, 1), (7, 2)]), v[pl.ds(MID, 512), :])

    await_chunks(q7, 4, 10, owns_47)

    out_ref[:16, :] += nn(joint([(4, 0), (5, 0)]), u[pl.ds(TOP7, 256), :])
    out_ref[16:, :] += nn(joint([(6, 0), (7, 0)]), v[pl.ds(TOP7, 256), :])

    await_chunks(q8, 4, 11, owns_8)

    out_ref[:16, :] += nn(joint([(k, 0) for k in range(4)]), u[pl.ds(TOP8, 512), :])
    out_ref[16:, :] += nn(joint([(k, 1) for k in range(4)]), v[pl.ds(TOP8, 512), :])

    wait(got.at[pl.ds(0, 5)], s1.at[0])
    wait(low0, sl)

    @pl.when(jnp.logical_not(owns))
    def _():
        wait(got.at[0], s1.at[1])
        wait(q7.at[pl.ds(0, 2)], s1.at[1])

    @pl.when(owns_8)
    def _():
        wait(got.at[0], s1.at[1])
        wait(q8, s2.at[0])
        wait(got.at[pl.ds(0, 10)], s3.at[3])

    @pl.when(owns_47)
    def _():
        wait(q7.at[pl.ds(0, 2)], s1.at[1])
        wait(q7, s2.at[1])
        wait(got.at[pl.ds(0, 10)], s3.at[1])
        wait(got.at[pl.ds(0, 5)], s3.at[2])

    mid_levels(lambda n: wait(qm.at[pl.ds(0, n)], s2.at[2]))

    @pl.when(zc < 3)
    def _():
        wait(q7.at[pl.ds(0, 2)], s1.at[2])
        wait(got.at[pl.ds(0, 5)], s3.at[0])

    @pl.when(zc >= 3)
    def _():
        wait(q7.at[pl.ds(0, 3)], s1.at[2])


def shards(coords, probes, u_bases, v_bases):
    tile = (16, 128)
    operands = [
        pltpu.with_memory_space_constraint(a, pltpu.HBM) for a in (coords, probes, u_bases, v_bases)
    ]
    both = pl.pallas_call(
        kernel,
        out_shape=jax.ShapeDtypeStruct((32, POINTS_HERE), F32),
        in_specs=[pl.BlockSpec(memory_space=pl.ANY)] * 4,
        out_specs=pl.BlockSpec(memory_space=pltpu.VMEM),
        scratch_shapes=[
            pltpu.VMEM((2, POINTS_HERE), jnp.int32),
            pltpu.VMEM((16, POINTS_HERE), jnp.int32),
            pltpu.VMEM((16, POINTS_HERE), BF16),
            pltpu.VMEM((RANKS, POINTS_HERE), BF16),
            pltpu.VMEM((RANKS, POINTS_HERE), BF16),
            pltpu.VMEM((8, 3) + tile, BF16),
            pltpu.VMEM(tile, BF16),
            pltpu.VMEM((16, 3) + tile, BF16),
            pltpu.VMEM((3,) + tile, BF16),
            pltpu.VMEM((16, 2) + tile, BF16),
            pltpu.VMEM((8,) + tile, BF16),
            pltpu.VMEM((4, 2) + tile, BF16),
            pltpu.VMEM((8,) + tile, BF16),
            pltpu.VMEM((8, 3) + tile, BF16),
            pltpu.VMEM(tile, BF16),
            pltpu.SemaphoreType.DMA((10,)),
            pltpu.SemaphoreType.DMA((3,)),
            pltpu.SemaphoreType.DMA((3,)),
            pltpu.SemaphoreType.DMA((4,)),
            pltpu.SemaphoreType.DMA,
            pltpu.SemaphoreType.DMA((12,)),
        ],
        compiler_params=pltpu.CompilerParams(
            collective_id=0, has_side_effects=True, vmem_limit_bytes=VMEM_BYTES
        ),
    )(*operands)
    return both[:16], both[16:]


def solution(mesh):
    return jax.shard_map(
        shards,
        mesh=mesh,
        in_specs=(P(None, "pts"), P(None, "pts"), P(None, "pts"), P(None, "pts")),
        out_specs=(P(None, "pts"), P(None, "pts")),
        check_vma=False,
    )
```

time: 328 us -> 31.4 us (0.10); the launches traced: 323 us -> 31.2 us
  starting transfers between devices: 306 us -> 0 us
  Pallas kernels: 0 us -> 30 us
  waiting for transfers between devices: 6.05 us -> 0 us
  matrix products: 5.33 us -> 0 us
    ppermute x90 -> x0, starting transfers between devices: 306 us -> none  [partner(): lax.ppermute(x, axis, [(i, i ^ 1 << apart) for i in range(lax.axis_size(a...]
    pallas_call x0 -> x1, Pallas kernels: none -> 30 us  [shards(): pl.pallas_call(kernel, out_shape=jax.ShapeDtypeStruct((32, POINTS_HERE),...]
    ppermute x90 -> x0, waiting for transfers between devices: 6.05 us -> none  [partner(): lax.ppermute(x, axis, [(i, i ^ 1 << apart) for i in range(lax.axis_size(a...]
    dot_general x9 -> x0, matrix products: 5.33 us -> none  [the longest x1 1.91 us: shards(): lax.dot_general(sign_rows, cross_u, contract_dims, preferred_element_type...]
  transfers between devices with their start and end apart: 90 -> 0, of which waited for: 4 -> 0; matrix products, arithmetic and copies ran while one was open for 1% -> 0% of each run, Pallas kernels for 0% -> 0%
where the time goes in v3:
time: 31.4 us; the launch traced here: 31.2 us
  Pallas kernels  30 us (96%)
  between operations  0.64 us (2%)
  local copies, waits for them, and re-layouts  0.63 us (2%)
    pallas_call x1, Pallas kernels, shards(): pl.pallas_call(kernel, out_shape=jax.ShapeDtypeStruct((32, POINTS_HERE),...  30 us
    slice x1, local copies, waits for them, and re-layouts, shards(): return (both[:16], both[16:])  0.63 us

profile of v3, /device:TPU:1, one launch (start us, length us, event | category | flops | bytes accessed | tf_op | source)
XLA Modules:
  0.0 31.2 jit_solution(8059871161443068388)
XLA Ops:
  0.6 30.0 %shard_map.59 = f32[32,512]{1,0:T(8,128)S(1)} custom-call(s32[2,512]{1,0:T(2,128)} %coords_hbm.1, s32[16,512]{1,0:T(8,128)} %probes_hbm.1, bf16[1600,512]{1,0:T(8,128)(2,1)} %u_hbm.1, bf16[1600,512]{1,0:T(8,128)(2,1)} %v_hbm.1), custom_call_target="tpu_custom_call" | custom-call | tf_op jit(solution)/shard_map/pallas_call | solution.py:390
  30.6 0.6 %fusion = (f32[16,512]{1,0:T(8,128)}, f32[16,512]{1,0:T(8,128)}) fusion(f32[32,512]{1,0:T(8,128)S(1)} %shard_map.59), kind=kLoop, calls=%fused_computation | loop fusion | bytes 131072 | tf_op jit(solution)/shard_map/slice | solution.py:422

commit v4 on v0

v4 whole, which is shorter than its diff:
```python
import jax
import jax.numpy as jnp
from jax import lax
from jax.experimental import pallas as pl
from jax.experimental.pallas import tpu as pltpu
from jax.sharding import PartitionSpec as P

MESH = pl.DeviceIdType.MESH
F32 = jnp.float32
BF16 = jnp.bfloat16

LEAF = 256
VMEM_BYTES = 32 * 1024 * 1024
POINTS_HERE = 512
RANKS = 1600
LOW, MID, TOP67, TOP8 = 0, 320, 576, 1088

cell_units = 16.0
length_scale = 4.0
root_three = 1.7320508075688772
nugget = 0.1


def device(x, y, z, c):
    return ((x * 8 + y) * 8 + z) * 2 + c


def nt(a, b):
    return lax.dot_general(a, b, (((1,), (1,)), ((), ())), preferred_element_type=F32)


def nn(a, b):
    return jnp.dot(a, b, preferred_element_type=F32)


def send(src, dst, send_sem, recv_sem, to):
    pltpu.make_async_remote_copy(
        src_ref=src,
        dst_ref=dst,
        send_sem=send_sem,
        recv_sem=recv_sem,
        device_id=(to,),
        device_id_type=MESH,
    ).start()


def wait(ref, sem):
    pltpu.make_async_copy(ref, ref, sem).wait()


def matern(spots, leaf):
    cols = spots[:, leaf * LEAF : (leaf + 1) * LEAF]
    tall = jnp.transpose(cols)
    delta_x = tall[:, 0:1] - cols[0:1, :]
    delta_y = tall[:, 1:2] - cols[1:2, :]
    scaled = (root_three / length_scale) * jnp.sqrt(delta_x * delta_x + delta_y * delta_y)
    row = lax.broadcasted_iota(jnp.int32, (LEAF, LEAF), 0)
    col = lax.broadcasted_iota(jnp.int32, (LEAF, LEAF), 1)
    block = (1.0 + scaled) * jnp.exp(-scaled) + jnp.where(row == col, nugget, 0.0)
    return block.astype(BF16)


def kernel(
    coords_hbm, probes_hbm, u_hbm, v_hbm, out_ref,
    coords, probes, signs, w,
    give, take, snd, low0, got, mine, q8, q7, q6, q45, low_out, fin, fin0,
    load, sent, rx, rs,
):
    me = lax.axis_index("pts")
    c = me % 2
    z = (me // 2) % 8
    y = (me // 16) % 8
    x = me // 128
    core0 = c == 0
    owns = z < 4
    owns_8 = z < 2
    owns_67 = jnp.logical_and(z >= 2, z < 4)
    half = 2 - (x // 2) * 2
    beside = x + 1 - 2 * (x % 2)
    partner = device(x, y, z, 1 - c)
    v, u = w.at[0], w.at[1]
    other, own = w.at[1 - c], w.at[c]

    def chunks(n):
        return q8.at[pl.ds(0, n // 2)] if n % 2 == 0 else q8.at[pl.ds(0, n), 0]

    pieces = [(TOP8, 512), (TOP67, 512), (LOW, 576)]

    def load_bases(sources):
        for i, rows in enumerate(pieces):
            for (src, dst), sem in zip(sources, ((0, 1), (1, 2), (3, 3))[i]):
                pltpu.make_async_copy(
                    src.at[pl.ds(*rows)], dst.at[pl.ds(*rows)], load.at[sem]
                ).start()

    probes_in = pltpu.make_async_copy(probes_hbm, probes, load.at[0])
    probes_in.start()
    coords_in = pltpu.make_async_copy(coords_hbm, coords, load.at[3])

    @pl.when(core0)
    def _():
        load_bases([(u_hbm, u), (v_hbm, v)])

    @pl.when(c == 1)
    def _():
        load_bases([(v_hbm, v), (u_hbm, u)])

    coords_in.start()

    def await_rows(piece, sem):
        wait(v.at[pl.ds(*pieces[piece])], load.at[sem])

    barrier = pltpu.get_barrier_semaphore()

    def greet(to):
        pl.semaphore_signal(barrier, inc=1, device_id=(to,), device_id_type=MESH)

    greet(partner)

    @pl.when(owns)
    def _():
        for j in range(1, 8):
            greet(device(x, y, (z + j) % 8, c))

    @pl.when(owns_8)
    def _():
        for h in range(2):
            for j in range(8):
                greet(device(half + h, j, z, c))

    def siblings(n):
        node = y // n
        first = (node + 1 - 2 * (node % 2)) * n
        return [device(x, first + j, z, c) for j in range(n)]

    @pl.when(z == 1)
    def _():
        for to in siblings(1) + siblings(2):
            greet(to)

    @pl.when(z == 2)
    def _():
        for j in range(8):
            greet(device(beside, j, z, c))

    @pl.when(z == 3)
    def _():
        for to in siblings(4):
            greet(to)

    probes_in.wait()
    await_rows(0, 0)
    signs[...] = (2 * probes[...] - 1).astype(BF16)

    def coefs(bases, first, count):
        return nt(signs[...], bases[pl.ds(first, count), :])

    def lanes(part, k):
        return part[:, k * 128 : (k + 1) * 128]

    def hand_over(first, part, count, i):
        for k in range(count):
            give[first + k] = lanes(part, k)
        rows = pl.ds(first, count)
        send(give.at[rows], take.at[rows], sent, rx.at[i], partner)

    other_8 = coefs(other, TOP8, 512)

    for place, count in enumerate((20, 23, 12, 8)):
        @pl.when(z == place)
        def _():
            pl.semaphore_wait(barrier, count)

    @pl.when(jnp.logical_not(owns))
    def _():
        pl.semaphore_wait(barrier, 5)

    hand_over(0, other_8, 4, 0)
    await_rows(0, 1)
    await_rows(1, 1)
    hand_over(4, coefs(other, TOP67, 512), 4, 1)

    def to_owner(place, rows, recv_sem):
        @pl.when(z != place)
        def _():
            send(
                snd.at[place, rows], got.at[z, rows], sent, rs.at[recv_sem],
                device(x, y, place, c),
            )

        @pl.when(z == place)
        def _():
            got[place, rows] = snd[place, rows]

    own_8 = coefs(own, TOP8, 512)

    wait(take.at[pl.ds(0, 4)], rx.at[0])
    for k in range(4):
        snd[k // 2, k % 2] = (lanes(own_8, k) + take[k]).astype(BF16)
    for place in range(2):
        to_owner(place, pl.ds(0, 2), 0)

    await_rows(1, 2)
    own_67 = coefs(own, TOP67, 512)

    wait(take.at[pl.ds(4, 4)], rx.at[1])
    for k in range(4):
        snd[3 - k // 2, k % 2] = (lanes(own_67, k) + take[4 + k]).astype(BF16)
    for place in (2, 3):
        to_owner(place, pl.ds(0, 2), 0)

    coords_in.wait()
    await_rows(2, 3)
    await_rows(2, 3)
    spots = coords[...].astype(F32) / cell_units
    for leaf in range(2):
        cols = pl.ds(leaf * LEAF, LEAF)
        across = pl.ds((1 - leaf) * LEAF, LEAF)
        near = nn(signs[:, cols], matern(spots, leaf))
        coef_f = nt(signs[:, across], v[pl.ds(0, 64), across]).astype(BF16)
        coef_t = nt(signs[:, across], u[pl.ds(0, 64), across]).astype(BF16)
        out_ref[:16, cols] = near + nn(coef_f, u[pl.ds(0, 64), cols])
        out_ref[16:, cols] = near + nn(coef_t, v[pl.ds(0, 64), cols])

    other_low = coefs(other, 64, 512)
    hand_over(8, other_low, 4, 2)
    own_low = coefs(own, 64, 512)
    f_0 = jnp.where(core0, own_low[:, :64], other_low[:, :64])
    t_0 = jnp.where(core0, other_low[:, :64], own_low[:, :64])
    low0[...] = jnp.concatenate([f_0, t_0], axis=1).astype(BF16)
    send(low0, fin0, sent, rs.at[2], partner)
    wait(take.at[pl.ds(8, 4)], rx.at[2])
    for k, (place, row) in enumerate(((0, 2), (1, 2), (1, 3), (1, 4))):
        snd[place, row] = (lanes(own_low, k) + take[8 + k]).astype(BF16)
    to_owner(1, pl.ds(2, 3), 1)
    to_owner(0, pl.ds(2, 1), 1)

    def total(parts):
        return sum(part.astype(F32) for part in parts)

    @pl.when(owns)
    def _():
        wait(q8.at[pl.ds(0, 7)], rs.at[0])
        for a in range(2):
            mine[a] = total(got[k, a] for k in range(8)).astype(BF16)

    @pl.when(owns_8)
    def _():
        for j in (0, 1, 7, 2, 6, 3, 5, 4):
            for h in range(2):
                to = device(half + h, j, z, c)
                send(mine.at[pl.ds(0, 2)], q8.at[(x % 2) * 8 + y], sent, rs.at[3], to)

    @pl.when(z == 2)
    def _():
        for j in (0, 1, 7, 2, 6, 3, 5, 4):
            send(mine.at[pl.ds(0, 2)], q7.at[y], sent, rs.at[3], device(beside, j, z, c))

    @pl.when(z == 3)
    def _():
        for to in siblings(4):
            send(mine.at[pl.ds(0, 2)], q6.at[y % 4], sent, rs.at[3], to)

    def hand_out_low(own_place, source, recv_sem):
        for place in (0, 1, 2, 3, 4, 5, 6, 7):
            if place == own_place:
                fin[c, own_place, 2] = source(place)[...]
                send(source(place), fin.at[c, own_place, 2], sent, rs.at[recv_sem], partner)
            else:
                for core in range(2):
                    to = device(x, y, place, core)
                    send(source(place), fin.at[c, own_place, 2], sent, rs.at[recv_sem], to)

    @pl.when(z == 0)
    def _():
        wait(chunks(7), rs.at[1])
        hand_out_low(0, lambda place: got.at[place ^ 1, 2], 2)

    @pl.when(z == 1)
    def _():
        wait(got.at[pl.ds(0, 7), pl.ds(0, 3)], rs.at[1])
        for a in (3, 4):
            mine[a] = total(got[k, a] for k in range(8)).astype(BF16)
        for to in siblings(1):
            send(mine.at[3], q45.at[0], sent, rs.at[4], to)
        for to in siblings(2):
            send(mine.at[4], q45.at[1 + y % 2], sent, rs.at[4], to)
        pairs = [total(got[2 * k + i, 2] for i in range(2)) for k in range(4)]
        quads = [pairs[0] + pairs[1], pairs[2] + pairs[3]]
        lane = lax.broadcasted_iota(jnp.int32, (16, 128), 1)
        for k in range(4):
            low_out[k] = jnp.where(lane < 64, pairs[k ^ 1], quads[1 - k // 2]).astype(BF16)
        hand_out_low(1, lambda place: low_out.at[place // 2], 2)

    def hand_out(own_place, rows, recv_sem, places):
        src = fin.at[c, own_place, rows]
        for place in places:
            if place == own_place:
                send(src, src, sent, rs.at[recv_sem], partner)
            else:
                for core in range(2):
                    to = device(x, y, place, core)
                    send(src, src, sent, rs.at[recv_sem], to)

    @pl.when(z == 1)
    def _():
        wait(q45, rs.at[4])
        fin[c, 1, 3] = q45[0]
        fin[c, 1, 4] = total(q45[1 + k] for k in range(2)).astype(BF16)
        hand_out(1, pl.ds(3, 2), 5, (0, 1, 2, 3, 7, 4, 6, 5))

    @pl.when(z == 2)
    def _():
        wait(q7, rs.at[3])
        for a in range(2):
            fin[c, 2, a] = total(q7[k, a] for k in range(8)).astype(BF16)
        hand_out(2, pl.ds(0, 2), 6, (0, 1, 2, 3, 7, 4, 6, 5))

    @pl.when(z == 3)
    def _():
        wait(q6, rs.at[3])
        for a in range(2):
            fin[c, 3, a] = total(q6[k, a] for k in range(4)).astype(BF16)
        hand_out(3, pl.ds(0, 2), 6, (0, 1, 2, 3, 7, 4, 6, 5))

    for own_place in range(2):
        @pl.when(z == own_place)
        def _():
            wait(q8, rs.at[3])
            for a in range(2):
                fin[c, own_place, a] = total(q8[k, a] for k in range(16)).astype(BF16)
            hand_out(own_place, pl.ds(0, 2), 7, (0, 1, 2, 3, 7, 4, 6, 5))

    def await_chunks(most, least, sem, is_own):
        @pl.when(is_own)
        def _():
            wait(chunks(least), rs.at[sem])

        @pl.when(jnp.logical_not(is_own))
        def _():
            wait(chunks(most), rs.at[sem])

    await_chunks(5, 4, 2, owns_8)
    low_f = jnp.concatenate([fin0[:, :64], fin[0, 0, 2][:, 64:], fin[0, 1, 2]], axis=1)
    low_t = jnp.concatenate([fin0[:, 64:], fin[1, 0, 2][:, 64:], fin[1, 1, 2]], axis=1)
    out_ref[:16, :] += nn(low_f, u[pl.ds(64, 256), :])
    out_ref[16:, :] += nn(low_t, v[pl.ds(64, 256), :])

    await_chunks(4, 2, 5, z == 1)

    def add(places, first):
        count = 128 * len(places)
        for kind, bases in ((0, u), (1, v)):
            coefs_here = jnp.concatenate([fin[kind, place, row] for place, row in places], axis=1)
            out_ref[kind * 16 : kind * 16 + 16, :] += nn(coefs_here, bases[pl.ds(first, count), :])

    add([(1, 3), (1, 4)], MID)

    await_chunks(8, 6, 6, owns_67)

    add([(3, 0), (3, 1), (2, 0), (2, 1)], TOP67)

    await_chunks(8, 6, 7, owns_8)

    add([(0, 0), (0, 1), (1, 0), (1, 1)], TOP8)

    wait(give, sent)

    def left(*sizes):
        for n in sizes:
            wait(chunks(n), sent)

    @pl.when(jnp.logical_not(owns))
    def _():
        left(13)

    @pl.when(z == 0)
    def _():
        left(10, 32, 15, 30)

    @pl.when(z == 1)
    def _():
        left(8, 32, 3, 15, 30, 30)

    @pl.when(z == 2)
    def _():
        left(11, 16, 30)

    @pl.when(z == 3)
    def _():
        left(11, 8, 30)


def shards(coords, probes, u_bases, v_bases):
    tile = (16, 128)
    operands = [
        pltpu.with_memory_space_constraint(a, pltpu.HBM) for a in (coords, probes, u_bases, v_bases)
    ]
    both = pl.pallas_call(
        kernel,
        out_shape=jax.ShapeDtypeStruct((32, POINTS_HERE), F32),
        in_specs=[pl.BlockSpec(memory_space=pl.ANY)] * 4,
        out_specs=pl.BlockSpec(memory_space=pltpu.VMEM),
        scratch_shapes=[
            pltpu.VMEM((2, POINTS_HERE), jnp.int32),
            pltpu.VMEM((16, POINTS_HERE), jnp.int32),
            pltpu.VMEM((16, POINTS_HERE), BF16),
            pltpu.VMEM((2, RANKS, POINTS_HERE), BF16),
            pltpu.VMEM((12,) + tile, F32),
            pltpu.VMEM((12,) + tile, F32),
            pltpu.VMEM((4, 5) + tile, BF16),
            pltpu.VMEM(tile, BF16),
            pltpu.VMEM((8, 5) + tile, BF16),
            pltpu.VMEM((5,) + tile, BF16),
            pltpu.VMEM((16, 2) + tile, BF16),
            pltpu.VMEM((8, 2) + tile, BF16),
            pltpu.VMEM((4, 2) + tile, BF16),
            pltpu.VMEM((3,) + tile, BF16),
            pltpu.VMEM((4,) + tile, BF16),
            pltpu.VMEM((2, 4, 5) + tile, BF16),
            pltpu.VMEM(tile, BF16),
            pltpu.SemaphoreType.DMA((4,)),
            pltpu.SemaphoreType.DMA,
            pltpu.SemaphoreType.DMA((3,)),
            pltpu.SemaphoreType.DMA((8,)),
        ],
        compiler_params=pltpu.CompilerParams(
            collective_id=0, has_side_effects=True, vmem_limit_bytes=VMEM_BYTES
        ),
    )(*operands)
    return both[:16], both[16:]


def solution(mesh):
    return jax.shard_map(
        shards,
        mesh=mesh,
        in_specs=(P(None, "pts"), P(None, "pts"), P(None, "pts"), P(None, "pts")),
        out_specs=(P(None, "pts"), P(None, "pts")),
        check_vma=False,
    )
```

time: 328 us -> 30.6 us (0.09); the launches traced: 323 us -> 30.4 us
  starting transfers between devices: 306 us -> 0 us
  Pallas kernels: 0 us -> 29.2 us
  waiting for transfers between devices: 6.05 us -> 0 us
  matrix products: 5.33 us -> 0 us
    ppermute x90 -> x0, starting transfers between devices: 306 us -> none  [partner(): lax.ppermute(x, axis, [(i, i ^ 1 << apart) for i in range(lax.axis_size(a...]
    pallas_call x0 -> x1, Pallas kernels: none -> 29.2 us  [shards(): pl.pallas_call(kernel, out_shape=jax.ShapeDtypeStruct((32, POINTS_HERE),...]
    ppermute x90 -> x0, waiting for transfers between devices: 6.05 us -> none  [partner(): lax.ppermute(x, axis, [(i, i ^ 1 << apart) for i in range(lax.axis_size(a...]
    dot_general x9 -> x0, matrix products: 5.33 us -> none  [the longest x1 1.91 us: shards(): lax.dot_general(sign_rows, cross_u, contract_dims, preferred_element_type...]
  transfers between devices with their start and end apart: 90 -> 0, of which waited for: 4 -> 0; matrix products, arithmetic and copies ran while one was open for 1% -> 0% of each run, Pallas kernels for 0% -> 0%
where the time goes in v4:
time: 30.6 us; the launch traced here: 30.4 us
  Pallas kernels  29.2 us (95%)
  between operations  0.64 us (2%)
  local copies, waits for them, and re-layouts  0.63 us (2%)
    pallas_call x1, Pallas kernels, shards(): pl.pallas_call(kernel, out_shape=jax.ShapeDtypeStruct((32, POINTS_HERE),...  29.2 us
    slice x1, local copies, waits for them, and re-layouts, shards(): return (both[:16], both[16:])  0.63 us

profile of v4, /device:TPU:1, one launch (start us, length us, event | category | flops | bytes accessed | tf_op | source)
XLA Modules:
  0.0 30.4 jit_solution(14409293116300856507)
XLA Ops:
  0.6 29.2 %shard_map.59 = f32[32,512]{1,0:T(8,128)S(1)} custom-call(s32[2,512]{1,0:T(2,128)} %coords_hbm.1, s32[16,512]{1,0:T(8,128)} %probes_hbm.1, bf16[1600,512]{1,0:T(8,128)(2,1)} %u_hbm.1, bf16[1600,512]{1,0:T(8,128)(2,1)} %v_hbm.1), custom_call_target="tpu_custom_call" | custom-call | tf_op jit(solution)/shard_map/pallas_call | solution.py:399
  29.8 0.6 %fusion = (f32[16,512]{1,0:T(8,128)}, f32[16,512]{1,0:T(8,128)}) fusion(f32[32,512]{1,0:T(8,128)S(1)} %shard_map.59), kind=kLoop, calls=%fused_computation | loop fusion | bytes 131072 | tf_op jit(solution)/shard_map/slice | solution.py:431

commit v5 on v4

--- a/solution.py
+++ b/solution.py
@@ -307,21 +307,21 @@
         wait(q45, rs.at[4])
         fin[c, 1, 3] = q45[0]
         fin[c, 1, 4] = total(q45[1 + k] for k in range(2)).astype(BF16)
-        hand_out(1, pl.ds(3, 2), 5, (0, 1, 2, 3, 7, 4, 6, 5))
+        hand_out(1, pl.ds(3, 2), 5, range(8))
 
     @pl.when(z == 2)
     def _():
         wait(q7, rs.at[3])
         for a in range(2):
             fin[c, 2, a] = total(q7[k, a] for k in range(8)).astype(BF16)
-        hand_out(2, pl.ds(0, 2), 6, (0, 1, 2, 3, 7, 4, 6, 5))
+        hand_out(2, pl.ds(0, 2), 6, range(6))
 
     @pl.when(z == 3)
     def _():
         wait(q6, rs.at[3])
         for a in range(2):
             fin[c, 3, a] = total(q6[k, a] for k in range(4)).astype(BF16)
-        hand_out(3, pl.ds(0, 2), 6, (0, 1, 2, 3, 7, 4, 6, 5))
+        hand_out(3, pl.ds(0, 2), 6, range(7))
 
     for own_place in range(2):
         @pl.when(z == own_place)
@@ -329,7 +329,7 @@
             wait(q8, rs.at[3])
             for a in range(2):
                 fin[c, own_place, a] = total(q8[k, a] for k in range(16)).astype(BF16)
-            hand_out(own_place, pl.ds(0, 2), 7, (0, 1, 2, 3, 7, 4, 6, 5))
+            hand_out(own_place, pl.ds(0, 2), 7, range(8 - 3 * own_place))
 
     def await_chunks(most, least, sem, is_own):
         @pl.when(is_own)
@@ -358,11 +358,23 @@
 
     await_chunks(8, 6, 6, owns_67)
 
+    @pl.when(z == 1)
+    def _():
+        hand_out(1, pl.ds(0, 2), 7, (5, 6, 7))
+
     add([(3, 0), (3, 1), (2, 0), (2, 1)], TOP67)
 
     await_chunks(8, 6, 7, owns_8)
 
     add([(0, 0), (0, 1), (1, 0), (1, 1)], TOP8)
+
+    @pl.when(z == 2)
+    def _():
+        hand_out(2, pl.ds(0, 2), 6, (6, 7))
+
+    @pl.when(z == 3)
+    def _():
+        hand_out(3, pl.ds(0, 2), 6, (7,))
 
     wait(give, sent)
 

time: 30.6 us -> 30.6 us (level)
  no operation moved by 1% of the time
where the time goes in v5:
time: 30.6 us; the launch traced here: 30.4 us
  Pallas kernels  29.2 us (95%)
  between operations  0.64 us (2%)
  local copies, waits for them, and re-layouts  0.63 us (2%)
    pallas_call x1, Pallas kernels, shards(): pl.pallas_call(kernel, out_shape=jax.ShapeDtypeStruct((32, POINTS_HERE),...  29.2 us
    slice x1, local copies, waits for them, and re-layouts, shards(): return (both[:16], both[16:])  0.63 us

profile of v5, /device:TPU:1, one launch (start us, length us, event | category | flops | bytes accessed | tf_op | source)
XLA Modules:
  0.0 30.4 jit_solution(891836748768530937)
XLA Ops:
  0.6 29.2 %shard_map.59 = f32[32,512]{1,0:T(8,128)S(1)} custom-call(s32[2,512]{1,0:T(2,128)} %coords_hbm.1, s32[16,512]{1,0:T(8,128)} %probes_hbm.1, bf16[1600,512]{1,0:T(8,128)(2,1)} %u_hbm.1, bf16[1600,512]{1,0:T(8,128)(2,1)} %v_hbm.1), custom_call_target="tpu_custom_call" | custom-call | tf_op jit(solution)/shard_map/pallas_call | solution.py:411
  29.8 0.6 %fusion = (f32[16,512]{1,0:T(8,128)}, f32[16,512]{1,0:T(8,128)}) fusion(f32[32,512]{1,0:T(8,128)S(1)} %shard_map.59), kind=kLoop, calls=%fused_computation | loop fusion | bytes 131072 | tf_op jit(solution)/shard_map/slice | solution.py:443

commit v6 on v5

--- a/solution.py
+++ b/solution.py
@@ -164,7 +164,7 @@
         rows = pl.ds(first, count)
         send(give.at[rows], take.at[rows], sent, rx.at[i], partner)
 
-    other_8 = coefs(other, TOP8, 512)
+    other_8 = coefs(other, TOP8 + 256, 256)
 
     for place, count in enumerate((20, 23, 12, 8)):
         @pl.when(z == place)
@@ -175,7 +175,8 @@
     def _():
         pl.semaphore_wait(barrier, 5)
 
-    hand_over(0, other_8, 4, 0)
+    hand_over(2, other_8, 2, 0)
+    hand_over(0, coefs(other, TOP8, 256), 2, 3)
     await_rows(0, 1)
     await_rows(1, 1)
     hand_over(4, coefs(other, TOP67, 512), 4, 1)
@@ -192,12 +193,11 @@
         def _():
             got[place, rows] = snd[place, rows]
 
-    own_8 = coefs(own, TOP8, 512)
-
-    wait(take.at[pl.ds(0, 4)], rx.at[0])
-    for k in range(4):
-        snd[k // 2, k % 2] = (lanes(own_8, k) + take[k]).astype(BF16)
-    for place in range(2):
+    for place, i in ((1, 0), (0, 3)):
+        own_8 = coefs(own, TOP8 + 256 * place, 256)
+        wait(take.at[pl.ds(2 * place, 2)], rx.at[i])
+        for k in range(2):
+            snd[place, k] = (lanes(own_8, k) + take[2 * place + k]).astype(BF16)
         to_owner(place, pl.ds(0, 2), 0)
 
     await_rows(1, 2)
@@ -267,7 +267,7 @@
                 fin[c, own_place, 2] = source(place)[...]
                 send(source(place), fin.at[c, own_place, 2], sent, rs.at[recv_sem], partner)
             else:
-                for core in range(2):
+                for core in (1, 0):
                     to = device(x, y, place, core)
                     send(source(place), fin.at[c, own_place, 2], sent, rs.at[recv_sem], to)
 
@@ -298,7 +298,7 @@
             if place == own_place:
                 send(src, src, sent, rs.at[recv_sem], partner)
             else:
-                for core in range(2):
+                for core in (1, 0):
                     to = device(x, y, place, core)
                     send(src, src, sent, rs.at[recv_sem], to)
 
@@ -329,7 +329,7 @@
             wait(q8, rs.at[3])
             for a in range(2):
                 fin[c, own_place, a] = total(q8[k, a] for k in range(16)).astype(BF16)
-            hand_out(own_place, pl.ds(0, 2), 7, range(8 - 3 * own_place))
+            hand_out(own_place, pl.ds(0, 2), 7 + own_place, range(8 - 3 * own_place))
 
     def await_chunks(most, least, sem, is_own):
         @pl.when(is_own)
@@ -360,13 +360,13 @@
 
     @pl.when(z == 1)
     def _():
-        hand_out(1, pl.ds(0, 2), 7, (5, 6, 7))
+        hand_out(1, pl.ds(0, 2), 8, (5, 6, 7))
 
     add([(3, 0), (3, 1), (2, 0), (2, 1)], TOP67)
 
-    await_chunks(8, 6, 7, owns_8)
-
-    add([(0, 0), (0, 1), (1, 0), (1, 1)], TOP8)
+    for place in range(2):
+        await_chunks(4, 2, 7 + place, z == place)
+        add([(place, 0), (place, 1)], TOP8 + 256 * place)
 
     @pl.when(z == 2)
     def _():
@@ -433,8 +433,8 @@
             pltpu.VMEM(tile, BF16),
             pltpu.SemaphoreType.DMA((4,)),
             pltpu.SemaphoreType.DMA,
-            pltpu.SemaphoreType.DMA((3,)),
-            pltpu.SemaphoreType.DMA((8,)),
+            pltpu.SemaphoreType.DMA((4,)),
+            pltpu.SemaphoreType.DMA((9,)),
         ],
         compiler_params=pltpu.CompilerParams(
             collective_id=0, has_side_effects=True, vmem_limit_bytes=VMEM_BYTES

time: 30.6 us -> 30.2 us (0.987)
  Pallas kernels: 29.2 us -> 28.8 us
    pallas_call x1, Pallas kernels: 29.2 us -> 28.8 us  [shards(): pl.pallas_call(kernel, out_shape=jax.ShapeDtypeStruct((32, POINTS_HERE),...]
where the time goes in v6:
time: 30.2 us; the launch traced here: 30 us
  Pallas kernels  28.8 us (95%)
  between operations  0.64 us (2%)
  local copies, waits for them, and re-layouts  0.63 us (2%)
    pallas_call x1, Pallas kernels, shards(): pl.pallas_call(kernel, out_shape=jax.ShapeDtypeStruct((32, POINTS_HERE),...  28.8 us
    slice x1, local copies, waits for them, and re-layouts, shards(): return (both[:16], both[16:])  0.63 us

profile of v6, /device:TPU:1, one launch (start us, length us, event | category | flops | bytes accessed | tf_op | source)
XLA Modules:
  0.0 30.0 jit_solution(13561500214655282489)
XLA Ops:
  0.6 28.8 %shard_map.59 = f32[32,512]{1,0:T(8,128)S(1)} custom-call(s32[2,512]{1,0:T(2,128)} %coords_hbm.1, s32[16,512]{1,0:T(8,128)} %probes_hbm.1, bf16[1600,512]{1,0:T(8,128)(2,1)} %u_hbm.1, bf16[1600,512]{1,0:T(8,128)(2,1)} %v_hbm.1), custom_call_target="tpu_custom_call" | custom-call | tf_op jit(solution)/shard_map/pallas_call | solution.py:411
  29.4 0.6 %fusion = (f32[16,512]{1,0:T(8,128)}, f32[16,512]{1,0:T(8,128)}) fusion(f32[32,512]{1,0:T(8,128)S(1)} %shard_map.59), kind=kLoop, calls=%fused_computation | loop fusion | bytes 131072 | tf_op jit(solution)/shard_map/slice | solution.py:443

commit v7 on v6

--- a/solution.py
+++ b/solution.py
@@ -72,9 +72,15 @@
     y = (me // 16) % 8
     x = me // 128
     core0 = c == 0
-    owns = z < 4
-    owns_8 = z < 2
-    owns_67 = jnp.logical_and(z >= 2, z < 4)
+    core1 = c == 1
+    zc = z * 2 + c
+    owns = jnp.logical_and(core1, z < 4)
+    owns_8 = jnp.logical_and(core1, z < 2)
+    owns_67 = jnp.logical_and(owns, z >= 2)
+
+    def at(place):
+        return jnp.logical_and(core1, z == place)
+
     half = 2 - (x // 2) * 2
     beside = x + 1 - 2 * (x % 2)
     partner = device(x, y, z, 1 - c)
@@ -82,7 +88,9 @@
     other, own = w.at[1 - c], w.at[c]
 
     def chunks(n):
-        return q8.at[pl.ds(0, n // 2)] if n % 2 == 0 else q8.at[pl.ds(0, n), 0]
+        if n % 4 == 0:
+            return q8.at[pl.ds(0, n // 4)]
+        return q8.at[pl.ds(0, n // 2), 0] if n % 2 == 0 else q8.at[pl.ds(0, n), 0, 0]
 
     pieces = [(TOP8, 512), (TOP67, 512), (LOW, 576)]
 
@@ -119,8 +127,9 @@
 
     @pl.when(owns)
     def _():
-        for j in range(1, 8):
-            greet(device(x, y, (z + j) % 8, c))
+        for j in range(1, 16):
+            o = (zc + j) % 16
+            greet(device(x, y, o // 2, o % 2))
 
     @pl.when(owns_8)
     def _():
@@ -133,17 +142,17 @@
         first = (node + 1 - 2 * (node % 2)) * n
         return [device(x, first + j, z, c) for j in range(n)]
 
-    @pl.when(z == 1)
+    @pl.when(at(1))
     def _():
         for to in siblings(1) + siblings(2):
             greet(to)
 
-    @pl.when(z == 2)
+    @pl.when(at(2))
     def _():
         for j in range(8):
             greet(device(beside, j, z, c))
 
-    @pl.when(z == 3)
+    @pl.when(at(3))
     def _():
         for to in siblings(4):
             greet(to)
@@ -167,7 +176,7 @@
     other_8 = coefs(other, TOP8 + 256, 256)
 
     for place, count in enumerate((20, 23, 12, 8)):
-        @pl.when(z == place)
+        @pl.when(at(place))
         def _():
             pl.semaphore_wait(barrier, count)
 
@@ -182,16 +191,16 @@
     hand_over(4, coefs(other, TOP67, 512), 4, 1)
 
     def to_owner(place, rows, recv_sem):
-        @pl.when(z != place)
+        @pl.when(jnp.logical_not(at(place)))
         def _():
             send(
-                snd.at[place, rows], got.at[z, rows], sent, rs.at[recv_sem],
-                device(x, y, place, c),
+                snd.at[place, rows], got.at[z, rows, c], sent, rs.at[recv_sem],
+                device(x, y, place, 1),
             )
 
-        @pl.when(z == place)
+        @pl.when(at(place))
         def _():
-            got[place, rows] = snd[place, rows]
+            got[place, rows, 1] = snd[place, rows]
 
     for place, i in ((1, 0), (0, 3)):
         own_8 = coefs(own, TOP8 + 256 * place, 256)
@@ -232,17 +241,22 @@
     wait(take.at[pl.ds(8, 4)], rx.at[2])
     for k, (place, row) in enumerate(((0, 2), (1, 2), (1, 3), (1, 4))):
         snd[place, row] = (lanes(own_low, k) + take[8 + k]).astype(BF16)
-    to_owner(1, pl.ds(2, 3), 1)
+    to_owner(1, pl.ds(3, 2), 1)
+    to_owner(1, pl.ds(2, 1), 9)
     to_owner(0, pl.ds(2, 1), 1)
 
     def total(parts):
         return sum(part.astype(F32) for part in parts)
 
+    def add_up(into, row, parts):
+        for kind in range(2):
+            into[row, kind] = total(part[kind] for part in parts).astype(BF16)
+
     @pl.when(owns)
     def _():
-        wait(q8.at[pl.ds(0, 7)], rs.at[0])
+        wait(chunks(30), rs.at[0])
         for a in range(2):
-            mine[a] = total(got[k, a] for k in range(8)).astype(BF16)
+            add_up(mine, a, [got.at[k, a] for k in range(8)])
 
     @pl.when(owns_8)
     def _():
@@ -251,12 +265,12 @@
                 to = device(half + h, j, z, c)
                 send(mine.at[pl.ds(0, 2)], q8.at[(x % 2) * 8 + y], sent, rs.at[3], to)
 
-    @pl.when(z == 2)
+    @pl.when(at(2))
     def _():
         for j in (0, 1, 7, 2, 6, 3, 5, 4):
             send(mine.at[pl.ds(0, 2)], q7.at[y], sent, rs.at[3], device(beside, j, z, c))
 
-    @pl.when(z == 3)
+    @pl.when(at(3))
     def _():
         for to in siblings(4):
             send(mine.at[pl.ds(0, 2)], q6.at[y % 4], sent, rs.at[3], to)
@@ -264,36 +278,38 @@
     def hand_out_low(own_place, source, recv_sem):
         for place in (0, 1, 2, 3, 4, 5, 6, 7):
             if place == own_place:
-                fin[c, own_place, 2] = source(place)[...]
-                send(source(place), fin.at[c, own_place, 2], sent, rs.at[recv_sem], partner)
+                fin[own_place, 2] = source(place)[...]
+                send(source(place), fin.at[own_place, 2], sent, rs.at[recv_sem], partner)
             else:
                 for core in (1, 0):
                     to = device(x, y, place, core)
-                    send(source(place), fin.at[c, own_place, 2], sent, rs.at[recv_sem], to)
-
-    @pl.when(z == 0)
-    def _():
-        wait(chunks(7), rs.at[1])
+                    send(source(place), fin.at[own_place, 2], sent, rs.at[recv_sem], to)
+
+    @pl.when(at(0))
+    def _():
+        wait(chunks(15), rs.at[1])
         hand_out_low(0, lambda place: got.at[place ^ 1, 2], 2)
 
-    @pl.when(z == 1)
-    def _():
-        wait(got.at[pl.ds(0, 7), pl.ds(0, 3)], rs.at[1])
+    @pl.when(at(1))
+    def _():
+        wait(chunks(30), rs.at[1])
+        wait(chunks(15), rs.at[9])
         for a in (3, 4):
-            mine[a] = total(got[k, a] for k in range(8)).astype(BF16)
+            add_up(mine, a, [got.at[k, a] for k in range(8)])
         for to in siblings(1):
             send(mine.at[3], q45.at[0], sent, rs.at[4], to)
         for to in siblings(2):
             send(mine.at[4], q45.at[1 + y % 2], sent, rs.at[4], to)
-        pairs = [total(got[2 * k + i, 2] for i in range(2)) for k in range(4)]
-        quads = [pairs[0] + pairs[1], pairs[2] + pairs[3]]
         lane = lax.broadcasted_iota(jnp.int32, (16, 128), 1)
-        for k in range(4):
-            low_out[k] = jnp.where(lane < 64, pairs[k ^ 1], quads[1 - k // 2]).astype(BF16)
+        for kind in range(2):
+            pairs = [total(got[2 * k + i, 2, kind] for i in range(2)) for k in range(4)]
+            quads = [pairs[0] + pairs[1], pairs[2] + pairs[3]]
+            for k in range(4):
+                low_out[k, kind] = jnp.where(lane < 64, pairs[k ^ 1], quads[1 - k // 2]).astype(BF16)
         hand_out_low(1, lambda place: low_out.at[place // 2], 2)
 
     def hand_out(own_place, rows, recv_sem, places):
-        src = fin.at[c, own_place, rows]
+        src = fin.at[own_place, rows]
         for place in places:
             if place == own_place:
                 send(src, src, sent, rs.at[recv_sem], partner)
@@ -302,77 +318,78 @@
                     to = device(x, y, place, core)
                     send(src, src, sent, rs.at[recv_sem], to)
 
-    @pl.when(z == 1)
+    @pl.when(at(1))
     def _():
         wait(q45, rs.at[4])
-        fin[c, 1, 3] = q45[0]
-        fin[c, 1, 4] = total(q45[1 + k] for k in range(2)).astype(BF16)
+        fin[1, 3] = q45[0]
+        add_up(fin.at[1], 4, [q45.at[1 + k] for k in range(2)])
         hand_out(1, pl.ds(3, 2), 5, range(8))
 
-    @pl.when(z == 2)
+    @pl.when(at(2))
     def _():
         wait(q7, rs.at[3])
         for a in range(2):
-            fin[c, 2, a] = total(q7[k, a] for k in range(8)).astype(BF16)
+            add_up(fin.at[2], a, [q7.at[k, a] for k in range(8)])
         hand_out(2, pl.ds(0, 2), 6, range(6))
 
-    @pl.when(z == 3)
+    @pl.when(at(3))
     def _():
         wait(q6, rs.at[3])
         for a in range(2):
-            fin[c, 3, a] = total(q6[k, a] for k in range(4)).astype(BF16)
+            add_up(fin.at[3], a, [q6.at[k, a] for k in range(4)])
         hand_out(3, pl.ds(0, 2), 6, range(7))
 
     for own_place in range(2):
-        @pl.when(z == own_place)
+        @pl.when(at(own_place))
         def _():
             wait(q8, rs.at[3])
             for a in range(2):
-                fin[c, own_place, a] = total(q8[k, a] for k in range(16)).astype(BF16)
+                add_up(fin.at[own_place], a, [q8.at[k, a] for k in range(16)])
             hand_out(own_place, pl.ds(0, 2), 7 + own_place, range(8 - 3 * own_place))
 
     def await_chunks(most, least, sem, is_own):
-        @pl.when(is_own)
-        def _():
-            wait(chunks(least), rs.at[sem])
+        if least:
+            @pl.when(is_own)
+            def _():
+                wait(chunks(least), rs.at[sem])
 
         @pl.when(jnp.logical_not(is_own))
         def _():
             wait(chunks(most), rs.at[sem])
 
-    await_chunks(5, 4, 2, owns_8)
-    low_f = jnp.concatenate([fin0[:, :64], fin[0, 0, 2][:, 64:], fin[0, 1, 2]], axis=1)
-    low_t = jnp.concatenate([fin0[:, 64:], fin[1, 0, 2][:, 64:], fin[1, 1, 2]], axis=1)
+    await_chunks(5, 3, 2, owns_8)
+    low_f = jnp.concatenate([fin0[:, :64], fin[0, 2, 0][:, 64:], fin[1, 2, 0]], axis=1)
+    low_t = jnp.concatenate([fin0[:, 64:], fin[0, 2, 1][:, 64:], fin[1, 2, 1]], axis=1)
     out_ref[:16, :] += nn(low_f, u[pl.ds(64, 256), :])
     out_ref[16:, :] += nn(low_t, v[pl.ds(64, 256), :])
 
-    await_chunks(4, 2, 5, z == 1)
+    await_chunks(4, 0, 5, at(1))
 
     def add(places, first):
         count = 128 * len(places)
         for kind, bases in ((0, u), (1, v)):
-            coefs_here = jnp.concatenate([fin[kind, place, row] for place, row in places], axis=1)
+            coefs_here = jnp.concatenate([fin[place, row, kind] for place, row in places], axis=1)
             out_ref[kind * 16 : kind * 16 + 16, :] += nn(coefs_here, bases[pl.ds(first, count), :])
 
     add([(1, 3), (1, 4)], MID)
 
-    await_chunks(8, 6, 6, owns_67)
-
-    @pl.when(z == 1)
+    await_chunks(8, 4, 6, owns_67)
+
+    @pl.when(at(1))
     def _():
         hand_out(1, pl.ds(0, 2), 8, (5, 6, 7))
 
     add([(3, 0), (3, 1), (2, 0), (2, 1)], TOP67)
 
     for place in range(2):
-        await_chunks(4, 2, 7 + place, z == place)
+        await_chunks(4, 0, 7 + place, at(place))
         add([(place, 0), (place, 1)], TOP8 + 256 * place)
 
-    @pl.when(z == 2)
+    @pl.when(at(2))
     def _():
         hand_out(2, pl.ds(0, 2), 6, (6, 7))
 
-    @pl.when(z == 3)
+    @pl.when(at(3))
     def _():
         hand_out(3, pl.ds(0, 2), 6, (7,))
 
@@ -386,21 +403,21 @@
     def _():
         left(13)
 
-    @pl.when(z == 0)
-    def _():
-        left(10, 32, 15, 30)
-
-    @pl.when(z == 1)
-    def _():
-        left(8, 32, 3, 15, 30, 30)
-
-    @pl.when(z == 2)
-    def _():
-        left(11, 16, 30)
-
-    @pl.when(z == 3)
-    def _():
-        left(11, 8, 30)
+    @pl.when(at(0))
+    def _():
+        left(10, 64, 30, 60)
+
+    @pl.when(at(1))
+    def _():
+        left(8, 64, 6, 30, 60, 60)
+
+    @pl.when(at(2))
+    def _():
+        left(11, 32, 60)
+
+    @pl.when(at(3))
+    def _():
+        left(11, 16, 60)
 
 
 def shards(coords, probes, u_bases, v_bases):
@@ -422,19 +439,19 @@
             pltpu.VMEM((12,) + tile, F32),
             pltpu.VMEM((4, 5) + tile, BF16),
             pltpu.VMEM(tile, BF16),
-            pltpu.VMEM((8, 5) + tile, BF16),
-            pltpu.VMEM((5,) + tile, BF16),
-            pltpu.VMEM((16, 2) + tile, BF16),
-            pltpu.VMEM((8, 2) + tile, BF16),
+            pltpu.VMEM((8, 5, 2) + tile, BF16),
+            pltpu.VMEM((5, 2) + tile, BF16),
+            pltpu.VMEM((16, 2, 2) + tile, BF16),
+            pltpu.VMEM((8, 2, 2) + tile, BF16),
+            pltpu.VMEM((4, 2, 2) + tile, BF16),
+            pltpu.VMEM((3, 2) + tile, BF16),
             pltpu.VMEM((4, 2) + tile, BF16),
-            pltpu.VMEM((3,) + tile, BF16),
-            pltpu.VMEM((4,) + tile, BF16),
-            pltpu.VMEM((2, 4, 5) + tile, BF16),
+            pltpu.VMEM((4, 5, 2) + tile, BF16),
             pltpu.VMEM(tile, BF16),
             pltpu.SemaphoreType.DMA((4,)),
             pltpu.SemaphoreType.DMA,
             pltpu.SemaphoreType.DMA((4,)),
-            pltpu.SemaphoreType.DMA((9,)),
+            pltpu.SemaphoreType.DMA((10,)),
         ],
         compiler_params=pltpu.CompilerParams(
             collective_id=0, has_side_effects=True, vmem_limit_bytes=VMEM_BYTES

time: 30.2 us -> 29.2 us (0.967)
  Pallas kernels: 28.8 us -> 27.8 us
    pallas_call x1, Pallas kernels: 28.8 us -> 27.8 us  [shards(): pl.pallas_call(kernel, out_shape=jax.ShapeDtypeStruct((32, POINTS_HERE),...]
where the time goes in v7:
time: 29.2 us; the launch traced here: 29 us
  Pallas kernels  27.8 us (95%)
  between operations  0.64 us (2%)
  local copies, waits for them, and re-layouts  0.63 us (2%)
    pallas_call x1, Pallas kernels, shards(): pl.pallas_call(kernel, out_shape=jax.ShapeDtypeStruct((32, POINTS_HERE),...  27.8 us
    slice x1, local copies, waits for them, and re-layouts, shards(): return (both[:16], both[16:])  0.63 us

profile of v7, /device:TPU:1, one launch (start us, length us, event | category | flops | bytes accessed | tf_op | source)
XLA Modules:
  0.0 29.0 jit_solution(7197483119292724816)
XLA Ops:
  0.6 27.8 %shard_map.59 = f32[32,512]{1,0:T(8,128)S(1)} custom-call(s32[2,512]{1,0:T(2,128)} %coords_hbm.1, s32[16,512]{1,0:T(8,128)} %probes_hbm.1, bf16[1600,512]{1,0:T(8,128)(2,1)} %u_hbm.1, bf16[1600,512]{1,0:T(8,128)(2,1)} %v_hbm.1), custom_call_target="tpu_custom_call" | custom-call | tf_op jit(solution)/shard_map/pallas_call | solution.py:428
  28.4 0.6 %fusion = (f32[16,512]{1,0:T(8,128)}, f32[16,512]{1,0:T(8,128)}) fusion(f32[32,512]{1,0:T(8,128)S(1)} %shard_map.59), kind=kLoop, calls=%fused_computation | loop fusion | bytes 131072 | tf_op jit(solution)/shard_map/slice | solution.py:460

commit v8 on v7

--- a/solution.py
+++ b/solution.py
@@ -190,11 +190,11 @@
     await_rows(1, 1)
     hand_over(4, coefs(other, TOP67, 512), 4, 1)
 
-    def to_owner(place, rows, recv_sem):
+    def to_owner(place, rows, recv_sem, split=0):
         @pl.when(jnp.logical_not(at(place)))
         def _():
             send(
-                snd.at[place, rows], got.at[z, rows, c], sent, rs.at[recv_sem],
+                snd.at[place, rows], got.at[z, rows, c], sent, rs.at[recv_sem + split * (1 - c)],
                 device(x, y, place, 1),
             )
 
@@ -207,7 +207,7 @@
         wait(take.at[pl.ds(2 * place, 2)], rx.at[i])
         for k in range(2):
             snd[place, k] = (lanes(own_8, k) + take[2 * place + k]).astype(BF16)
-        to_owner(place, pl.ds(0, 2), 0)
+        to_owner(place, pl.ds(0, 2), 0, 10)
 
     await_rows(1, 2)
     own_67 = coefs(own, TOP67, 512)
@@ -216,7 +216,7 @@
     for k in range(4):
         snd[3 - k // 2, k % 2] = (lanes(own_67, k) + take[4 + k]).astype(BF16)
     for place in (2, 3):
-        to_owner(place, pl.ds(0, 2), 0)
+        to_owner(place, pl.ds(0, 2), 0, 10)
 
     coords_in.wait()
     await_rows(2, 3)
@@ -252,18 +252,21 @@
         for kind in range(2):
             into[row, kind] = total(part[kind] for part in parts).astype(BF16)
 
-    @pl.when(owns)
-    def _():
-        wait(chunks(30), rs.at[0])
-        for a in range(2):
-            add_up(mine, a, [got.at[k, a] for k in range(8)])
-
-    @pl.when(owns_8)
-    def _():
-        for j in (0, 1, 7, 2, 6, 3, 5, 4):
-            for h in range(2):
-                to = device(half + h, j, z, c)
-                send(mine.at[pl.ds(0, 2)], q8.at[(x % 2) * 8 + y], sent, rs.at[3], to)
+    for kind, count, sem in ((1, 14, 0), (0, 16, 10)):
+        @pl.when(owns)
+        def _():
+            wait(chunks(count), rs.at[sem])
+            for a in range(2):
+                mine[a, kind] = total(got[k, a, kind] for k in range(8)).astype(BF16)
+
+        @pl.when(owns_8)
+        def _():
+            rows = pl.ds(0, 2)
+            for j in (0, 1, 7, 2, 6, 3, 5, 4):
+                for h in range(2):
+                    to = device(half + h, j, z, c)
+                    slot = q8.at[(x % 2) * 8 + y, rows, kind]
+                    send(mine.at[rows, kind], slot, sent, rs.at[3], to)
 
     @pl.when(at(2))
     def _():
@@ -451,7 +454,7 @@
             pltpu.SemaphoreType.DMA((4,)),
             pltpu.SemaphoreType.DMA,
             pltpu.SemaphoreType.DMA((4,)),
-            pltpu.SemaphoreType.DMA((10,)),
+            pltpu.SemaphoreType.DMA((11,)),
         ],
         compiler_params=pltpu.CompilerParams(
             collective_id=0, has_side_effects=True, vmem_limit_bytes=VMEM_BYTES

time: 29.2 us -> 29.3 us (level)
  no operation moved by 1% of the time
where the time goes in v8:
time: 29.3 us; the launch traced here: 29.2 us
  Pallas kernels  27.9 us (95%)
  between operations  0.64 us (2%)
  local copies, waits for them, and re-layouts  0.63 us (2%)
    pallas_call x1, Pallas kernels, shards(): pl.pallas_call(kernel, out_shape=jax.ShapeDtypeStruct((32, POINTS_HERE),...  27.9 us
    slice x1, local copies, waits for them, and re-layouts, shards(): return (both[:16], both[16:])  0.63 us

profile of v8, /device:TPU:1, one launch (start us, length us, event | category | flops | bytes accessed | tf_op | source)
XLA Modules:
  0.0 29.2 jit_solution(12633296433146452593)
XLA Ops:
  0.6 27.9 %shard_map.59 = f32[32,512]{1,0:T(8,128)S(1)} custom-call(s32[2,512]{1,0:T(2,128)} %coords_hbm.1, s32[16,512]{1,0:T(8,128)} %probes_hbm.1, bf16[1600,512]{1,0:T(8,128)(2,1)} %u_hbm.1, bf16[1600,512]{1,0:T(8,128)(2,1)} %v_hbm.1), custom_call_target="tpu_custom_call" | custom-call | tf_op jit(solution)/shard_map/pallas_call | solution.py:431
  28.6 0.6 %fusion = (f32[16,512]{1,0:T(8,128)}, f32[16,512]{1,0:T(8,128)}) fusion(f32[32,512]{1,0:T(8,128)S(1)} %shard_map.59), kind=kLoop, calls=%fused_computation | loop fusion | bytes 131072 | tf_op jit(solution)/shard_map/slice | solution.py:463
